TPU v7x, 32 devices: a whole 2x2x4 slice. The times are simulated.
32 devices in a mesh: seq: 8 (over z, x), seg: 4 (over y, core).
Axes of the slice: x: 2, y: 2, z: 4, core: 2. Of those that a mesh axis runs over, the one named last changes fastest.
Arguments:
- tokens: bfloat16 [4, 2048, 1024], P('seg', 'seq'), may hold values from -6 to 6
- starts: int32 [4, 4], P('seg'), may hold values from 0 to 2047, as said below
- norm_gain: bfloat16 [1024], P(('seq', 'seg')), may hold values from 0.099609375 to 1.8984375
- ema_delta: bfloat16 [1024, 16], P(('seq', 'seg'))
- ema_alpha: bfloat16 [1024, 16], P(('seq', 'seg'))
- ema_beta: bfloat16 [1024, 16], P(('seq', 'seg')), may hold values from -4 to 4
- ema_eta: bfloat16 [1024, 16], P(('seq', 'seg')), may hold values from -1 to 1
- ema_omega: bfloat16 [1024], P(('seq', 'seg')), may hold values from -4 to 4
- mix_weight: bfloat16 [1024, 4224], P('seq', 'seg'), may hold values from -0.1875 to 0.1875
- value_weight: bfloat16 [1024, 2048], P('seq', 'seg'), may hold values from -0.1875 to 0.1875
- qk_affine: bfloat16 [512], P(('seq', 'seg')), may hold values from -4 to 4
- out_weight: bfloat16 [2048, 1024], P('seq', 'seg'), may hold values from -0.25 to 0.25
- ffn_gain: bfloat16 [1024], P(('seq', 'seg')), may hold values from 0.099609375 to 1.8984375
- ffn_in: bfloat16 [1024, 4096], P('seq', 'seg'), may hold values from -0.1875 to 0.1875
- ffn_out: bfloat16 [4096, 1024], P('seq', 'seg'), may hold values from -0.09375 to 0.09375
- cotangent: bfloat16 [4, 2048, 1024], P('seg', 'seq'), may hold values from -6 to 6
Outputs:
- layer_out: bfloat16 [4, 2048, 1024], P('seg', 'seq')
- grad_tokens: bfloat16 [4, 2048, 1024], P('seg', 'seq')
- grad_norm_gain: float32 [1024], P(('seq', 'seg'))
- grad_ema_delta: float32 [1024, 16], P(('seq', 'seg'))
- grad_ema_alpha: float32 [1024, 16], P(('seq', 'seg'))
- grad_ema_beta: float32 [1024, 16], P(('seq', 'seg'))
- grad_ema_eta: float32 [1024, 16], P(('seq', 'seg'))
- grad_ema_omega: float32 [1024], P(('seq', 'seg'))
- grad_mix_weight: float32 [1024, 4224], P('seq', 'seg')
- grad_value_weight: float32 [1024, 2048], P('seq', 'seg')
- grad_qk_affine: float32 [512], P(('seq', 'seg'))
- grad_out_weight: float32 [2048, 1024], P('seq', 'seg')
- grad_ffn_gain: float32 [1024], P(('seq', 'seg'))
- grad_ffn_in: float32 [1024, 4096], P('seq', 'seg')
- grad_ffn_out: float32 [4096, 1024], P('seq', 'seg')
Inputs may be any that keep to these rules, and one draw needn't show every extreme that they name: Each row begins with 0 and never falls; document k of a segment runs from starts[k] to the next entry, the last one to the end of the segment.
All inputs are finite; a program needn't handle non-finite values.
Results may differ from a plain program's by a relative error of at most 0.02.
Values may be sent and summed in bfloat16 or wider, within the bound.
A program may use at most 512 MiB of HBM per device.

v0:
```python
import functools
import math

import jax
import jax.numpy as jnp
import numpy as np
from jax import lax
from jax.experimental import pallas as pl
from jax.experimental.pallas import tpu as pltpu
from jax.sharding import PartitionSpec as P

STRETCH = 128
epsilon = 1e-05
GATHER_LAG = (1, 1, 1, 1, 1)
SCATTER_LAG = (0, 1, 1, 1, 1)
GATHER_CUTS = (4, 2, 2, 4, 4)
SCATTER_CUTS = (4, 4, 2, 2, 4)

MESH = pl.DeviceIdType.MESH
ANY = pl.BlockSpec(memory_space=pl.ANY)


class Grid:
    def __init__(self, nq, ng):
        self.nq, self.ng = nq, ng
        self.nz = math.gcd(nq, 4)
        self.nx = nq // self.nz
        self.nc = math.gcd(ng, 2)
        self.ny = ng // self.nc

    def here(self):
        s, g = lax.axis_index("seq"), lax.axis_index("seg")
        return s // self.nx, lax.rem(s, self.nx), g // self.nc, lax.rem(g, self.nc)

    def peer(self, axis, d):
        z, x, y, c = self.here()
        if axis == "z":
            z = lax.rem(z + d, self.nz)
        if axis == "x":
            x = lax.rem(x + d, self.nx)
        if axis == "y":
            y = lax.rem(y + d, self.ny)
        if axis == "c":
            c = lax.rem(c + d, self.nc)
        return z, x, y, c

    def size(self, axis):
        return {"z": self.nz, "x": self.nx, "y": self.ny, "c": self.nc}[axis]

    def device(self, place):
        z, x, y, c = place
        return {"seq": z * self.nx + x, "seg": y * self.nc + c}

    def peers(self, axes):
        return [self.peer(a, d) for a in axes for d in range(1, self.size(a))]


def enter(grid, peers):
    barrier = pltpu.get_barrier_semaphore()
    for place in peers:
        pl.semaphore_signal(barrier, inc=1, device_id=grid.device(place), device_id_type=MESH)
    pl.semaphore_wait(barrier, len(peers))


class Sems:
    def __init__(self, send, recv):
        self.send, self.recv, self.used = send, recv, 0

    def take_index(self):
        self.used += 1
        return self.used - 1

    def take(self):
        i = self.take_index()
        return self.send.at[i], self.recv.at[i]


def gather_steps(grid, shapes, shards, wholes, own_sem, sems):
    n = len(shapes)
    z, x, y, c = grid.here()
    pending = []

    def push(src, dst, axis, d, arrives):
        s, r = sems.take()
        device = grid.device(grid.peer(axis, d))
        copy = pltpu.make_async_remote_copy(src, dst, s, r, device_id=device, device_id_type=MESH)
        copy.start()
        pending.append(copy)
        there = pltpu.make_async_remote_copy(arrives, arrives, s, r, device_id=device, device_id_type=MESH)
        return there.wait_recv

    def back(axis, d):
        return dict(zip("zxyc", grid.peer(axis, grid.size(axis) - d)))[axis]

    owns = []
    chunks = [(i, q) for i in range(n) for q in range(shapes[i][0] // 2)]
    core_waits = {}

    def core(k, view):
        core_waits.setdefault(k, []).extend(
            push(view(c), view(c), "c", d, view(back("c", d))) for d in range(1, grid.nc)
        )

    def stage_z(k, i, h):
        w = wholes[i]
        return [
            push(shards[i].at[h], w.at[y, c, z, x, h], "z", d, w.at[y, c, back("z", d), x, h])
            for d in range(1, grid.nz)
        ]

    def stage_two(k, i, h):
        w = wholes[i]
        src = w.at[y, c, :, x, h]
        if h % 2 == 0:
            waits = [push(src, src, "x", d, w.at[y, c, :, back("x", d), h]) for d in range(1, grid.nx)]
        else:
            waits = [push(src, src, "y", d, w.at[back("y", d), c, :, x, h]) for d in range(1, grid.ny)]
        core(k, lambda cc: w.at[y, cc, :, x, h])
        return waits

    def stage_three(k, i, h):
        w = wholes[i]
        if h % 2 == 0:
            src = w.at[y, c, :, :, h]
            waits = [push(src, src, "y", d, w.at[back("y", d), c, :, :, h]) for d in range(1, grid.ny)]
            for d in range(1, grid.nx):
                core(k, lambda cc: w.at[y, cc, :, back("x", d), h])
            return waits
        src = w.at[:, c, :, x, h]
        waits = [push(src, src, "x", d, w.at[:, c, :, back("x", d), h]) for d in range(1, grid.nx)]
        for d in range(1, grid.ny):
            core(k, lambda cc: w.at[back("y", d), cc, :, x, h])
        return waits

    def stage_last(k, i, h):
        w = wholes[i]
        if h % 2 == 0:
            for d in range(1, grid.ny):
                core(k, lambda cc: w.at[back("y", d), cc, :, :, h])
        else:
            for d in range(1, grid.nx):
                core(k, lambda cc: w.at[:, cc, :, back("x", d), h])

    def finish(waits):
        for wait in waits:
            wait()

    got = {}
    total = len(chunks)
    at = [0] * 5

    def advance(j):
        k = at[j]
        i, q = chunks[k]
        if j == 1 and q == 0:
            owns[i].wait()
        if j == 4:
            finish(core_waits[k])
            at[j] += 1
            return [i] if q + 1 == shapes[i][0] // 2 else []
        for h in (0, 1):
            if j:
                finish(got[k, h])
            got[k, h] = (stage_z, stage_two, stage_three, stage_last)[j](k, i, 2 * q + h)
        at[j] += 1
        return []

    advance(0)
    yield []
    for i in range(n):
        copy = pltpu.make_async_copy(shards[i], wholes[i].at[y, c, z, x], own_sem.at[i])
        copy.start()
        owns.append(copy)
    while at[4] < total:
        before = list(at)
        done = []
        for j in (1, 0, 2, 3, 4):
            if j == 0:
                go = at[0] < total and at[0] - at[1] < GATHER_LAG[0]
            else:
                go = at[j] < before[j - 1] and (before[j - 1] == total or before[j - 1] - at[j] >= GATHER_LAG[j])
            if go:
                done += advance(j)
        if at[4] == total:
            for copy in pending:
                copy.wait_send()
        yield done


def gather_plan(grid, shards, cuts):
    shapes, args, outs = [], [], []
    for w, q in zip(shards, cuts):
        k, n = w.shape
        q = max(1, min(q, k // 32))
        shapes.append((2 * q, k // (2 * q), n))
        args.append(w.reshape(shapes[-1]))
        outs.append(jax.ShapeDtypeStruct((grid.ny, grid.nc, grid.nz, grid.nx) + shapes[-1], w.dtype))
    per = (grid.nz - 1) + (grid.nx - 1) + (grid.ny - 1) + (grid.nc - 1) * (grid.nx + grid.ny)
    count = sum(s[0] for s in shapes) * per
    return shapes, args, outs, count


def scatter_steps(grid, shapes, terms, sums, scratch, own_sem, sems, ready=None):
    n = len(shapes)
    nz, nx, ny, nc = grid.nz, grid.nx, grid.ny, grid.nc
    own = [scratch[7 * i] for i in range(n)]
    one = [scratch[7 * i + 1] for i in range(n)]
    two_a = [scratch[7 * i + 2] for i in range(n)]
    two_b = [scratch[7 * i + 3] for i in range(n)]
    three_a = [scratch[7 * i + 4] for i in range(n)]
    three_b = [scratch[7 * i + 5] for i in range(n)]
    four = [scratch[7 * i + 6] for i in range(n)]
    z, x, y, c = grid.here()
    pending = []
    around = {(axis, d): grid.peer(axis, d) for axis in "zxyc" for d in range(1, grid.size(axis))}
    devices = {key: grid.device(place) for key, place in around.items()}

    def push(ends, axis, d):
        k = sems.take_index()

        def copy():
            return pltpu.make_async_remote_copy(
                *ends(), sems.send.at[k], sems.recv.at[k], device_id=devices[axis, d], device_id_type=MESH
            )

        copy().start()
        pending.append(lambda: copy().wait_send())
        return lambda: copy().wait_recv()

    def to(axis, d):
        return dict(zip("zxyc", around[axis, d]))[axis]

    def finish(waits):
        for wait in waits:
            wait()

    assert nc == 2

    def stage_one(i, q, h):
        return [push(lambda: (terms[i].at[:, to("c", 1), :, :, 2 * q + h], one[i].at[q, h]), "c", 1)]

    def load_own(i, q, h):
        def load():
            return pltpu.make_async_copy(terms[i].at[:, c, :, :, 2 * q + h], own[i].at[h], own_sem.at[i, h])

        load().start()
        return [lambda: load().wait()]

    def stage_two(i, q, h):
        mine = one[i].at[q, h]

        @pl.loop(0, ny * nz)
        def _(ab):
            a, b = ab // nz, lax.rem(ab, nz)
            for e in range(nx):
                mine[a, b, e] += own[i][h, a, b, e]

        if h == 0:
            return [
                push(lambda d=d: (one[i].at[q, h, to("y", d)], two_a[i].at[q, d - 1]), "y", d) for d in range(1, ny)
            ]
        return [
            push(lambda d=d: (one[i].at[q, h, :, :, to("x", d)], two_b[i].at[q, d - 1]), "x", d) for d in range(1, nx)
        ]

    def stage_three(i, q, h):
        mine = one[i].at[q, h]
        if h == 0:

            @pl.loop(0, nz)
            def _(b):
                for e in range(nx):
                    total = mine[y, b, e]
                    for d in range(ny - 1):
                        total += two_a[i][q, d, b, e]
                    mine[y, b, e] = total

            return [
                push(lambda d=d: (one[i].at[q, h, y, :, to("x", d)], three_a[i].at[q, d - 1]), "x", d)
                for d in range(1, nx)
            ]

        @pl.loop(0, nz)
        def _(b):
            for a in range(ny):
                total = mine[a, b, x]
                for d in range(nx - 1):
                    total += two_b[i][q, d, a, b]
                mine[a, b, x] = total

        return [
            push(lambda d=d: (one[i].at[q, h, to("y", d), :, x], three_b[i].at[q, d - 1]), "y", d)
            for d in range(1, ny)
        ]

    def stage_four(i, q, h):
        mine = one[i].at[q, h]
        came = three_a[i] if h == 0 else three_b[i]

        @pl.loop(0, nz)
        def _(b):
            total = mine[y, b, x]
            for d in range((nx if h == 0 else ny) - 1):
                total += came[q, d, b]
            mine[y, b, x] = total

        return [
            push(lambda d=d: (one[i].at[q, h, y, to("z", d), x], four[i].at[q, h, d - 1]), "z", d)
            for d in range(1, nz)
        ]

    def stage_last(i, q, h):
        total = one[i][q, h, y, z, x].astype(jnp.float32)
        for d in range(nz - 1):
            total += four[i][q, h, d].astype(jnp.float32)
        sums[i][2 * q + h] = total

    stages = [stage_one, stage_two, stage_three, stage_four, stage_last]
    chunks = [(i, q) for i in range(n) for q in range(shapes[i][0] // 2)]
    waits = {}
    total = len(chunks)
    at = [0] * len(stages)
    yield
    while at[-1] < total:
        there = total if ready is None else sum(1 for i, q in chunks if i < ready())
        before = [there] + at[:-1]
        fresh = None
        for j, stage in enumerate(stages):
            lag = SCATTER_LAG[j]
            if at[j] < before[j] and (before[j] == total or j == 0 or before[j] - at[j] >= lag):
                i, q = chunks[at[j]]
                for h in (0, 1):
                    if j:
                        finish(waits[i, q, h])
                    waits[i, q, h] = stage(i, q, h)
                if j == 0:
                    fresh = i, q
                at[j] += 1
            if j == 1 and fresh:
                for h in (0, 1):
                    waits[fresh[0], fresh[1], h] += load_own(*fresh, h)
        if at[-1] == total:
            finish(pending)
        yield


class SmallSum:
    def __init__(self, grid, small, total, seq_in, seg_in, send, recv):
        self.grid, self.small, self.total = grid, small, total
        self.seq_in, self.seg_in, self.send, self.recv = seq_in, seg_in, send, recv
        self.seq_peer, self.seg_peer = small_peers(grid)
        self.copies = []

    def push(self, src, dst, device):
        i = len(self.copies)
        copy = pltpu.make_async_remote_copy(
            src, dst, self.send.at[i], self.recv.at[i], device_id=device, device_id_type=MESH
        )
        copy.start()
        self.copies.append(copy)

    def start(self):
        nq, sq = self.grid.nq, lax.axis_index("seq")
        for d in range(1, nq):
            self.push(self.small.at[lax.rem(sq + d, nq)], self.seq_in.at[d - 1], self.seq_peer[d - 1])

    def middle(self):
        nq, ng = self.grid.nq, self.grid.ng
        total = self.small[lax.axis_index("seq")]
        for d in range(1, nq):
            self.copies[d - 1].wait_recv()
            total += self.seq_in[d - 1]
        self.total[...] = total
        for d in range(1, ng):
            self.push(self.total, self.seg_in.at[d - 1], self.seg_peer[d - 1])

    def end(self):
        nq, ng = self.grid.nq, self.grid.ng
        total = self.total[...]
        for d in range(1, ng):
            self.copies[nq + d - 2].wait_recv()
            total += self.seg_in[d - 1]
        for copy in self.copies:
            copy.wait_send()
        self.total[...] = total


def small_peers(grid):
    nq, ng = grid.nq, grid.ng
    s, g = lax.axis_index("seq"), lax.axis_index("seg")
    return (
        [{"seq": lax.rem(s + d, nq), "seg": g} for d in range(1, nq)],
        [{"seq": s, "seg": lax.rem(g + d, ng)} for d in range(1, ng)],
    )


def meet(peers):
    barrier = pltpu.get_barrier_semaphore()
    for place in peers:
        pl.semaphore_signal(barrier, inc=1, device_id=place, device_id_type=MESH)
    pl.semaphore_wait(barrier, len(peers))


def scatter_plan(grid, terms, cuts):
    nz, nx, ny = grid.nz, grid.nx, grid.ny
    shapes, outs, scratch = [], [], []
    for t, q in zip(terms, cuts):
        _, rows, n = t.shape
        if n < 128:
            rows, n = rows * n // 128, 128
        k = rows // grid.nq
        q = max(1, min(q, k // 32))
        kh = k // (2 * q)
        shapes.append((2 * q, kh, n))
        outs.append(jax.ShapeDtypeStruct((2 * q, kh, n), jnp.float32))
        b = t.dtype
        scratch += [
            pltpu.VMEM((2, ny, nz, nx, kh, n), b),
            pltpu.VMEM((q, 2, ny, nz, nx, kh, n), b),
            pltpu.VMEM((q, max(ny - 1, 1), nz, nx, kh, n), b),
            pltpu.VMEM((q, max(nx - 1, 1), ny, nz, kh, n), b),
            pltpu.VMEM((q, max(nx - 1, 1), nz, kh, n), b),
            pltpu.VMEM((q, max(ny - 1, 1), nz, kh, n), b),
            pltpu.VMEM((q, 2, max(nz - 1, 1), kh, n), b),
        ]
    per = (grid.nc - 1) + (nx - 1) + (ny - 1) + (nz - 1)
    count = per * sum(s[0] for s in shapes)
    return shapes, outs, scratch, count


def block_of(e, nq, blocks):
    return e * blocks // nq


def mix_kernel(grid, width, dims, shapes, *refs):
    n = len(shapes)
    shards, refs = refs[:n], refs[n:]
    tok, tile, alive, spans, mask, *refs = refs
    wholes, refs = refs[:n], refs[n:]
    (normed_out, active_out, x_out, mixed_out, carry_out, par_out, aff_out, probs_out, out_one_out, two_out, layer_out,
     proj_hbm, value_hbm, att_hbm, hin_hbm, hpre_hbm, ffn_hbm, act_hbm,
     proj, value_pre, att, hin, hpre, ffn_pre, act, values,
     tiles, table, bound, sends_t, recv_t, sends_b, recv_b, own_sem, flush_sem, load_sem, send, recv,
     *slots) = refs
    nq, ng = grid.nq, grid.ng
    rows = tok.shape[0]
    blocks = width // 128
    s = lax.axis_index("seq")
    seq_peer, seg_peer = small_peers(grid)
    meet(seq_peer + seg_peer)
    steps = gather_steps(grid, shapes, shards, wholes, own_sem, Sems(send, recv))

    done = set()

    def pump(count=1):
        for _ in range(count):
            done.update(next(steps, ()))

    copies = []
    for d in range(1, ng):
        copies.append(pltpu.make_async_remote_copy(
            tile, tiles.at[d - 1], sends_t.at[d - 1], recv_t.at[d - 1],
            device_id=seg_peer[d - 1], device_id_type=MESH))
        copies[-1].start()
    for copy in copies:
        copy.wait_recv()
    lanes = tile[...]
    for d in range(1, ng):
        lanes += tiles[d - 1]
    table[s] = lanes
    for d in range(1, nq):
        copies.append(pltpu.make_async_remote_copy(
            table.at[s], table.at[s], sends_t.at[ng + d - 2], recv_t.at[ng + d - 2],
            device_id=seq_peer[d - 1], device_id_type=MESH))
        copies[-1].start()
    pump()
    for d in range(1, nq):
        came = table.at[lax.rem(s + nq - d, nq)]
        pltpu.make_async_remote_copy(
            came, came, sends_t.at[ng + d - 2], recv_t.at[ng + d - 2],
            device_id=seq_peer[d - 1], device_id_type=MESH).wait_recv()
    count = 4 * dims + 3
    for b in range(blocks):
        mine = [e for e in range(nq) if block_of(e, nq, blocks) == b]
        whole = table[mine[0], 0:count]
        for e in mine[1:]:
            whole += table[e, 0:count]
        par_out[:, b, :] = whole
    aff = table[0, count : count + 4]
    for e in range(1, nq):
        aff += table[e, count : count + 4]
    aff_out[...] = aff

    pump()

    gain = [par_out[4 * dims, b : b + 1, :] for b in range(blocks)]
    step_rows = 32

    @pl.loop(0, rows // step_rows)
    def _(i):
        at = pl.ds(pl.multiple_of(i * step_rows, step_rows), step_rows)
        v = tok[at, :].astype(jnp.float32)
        r = lax.rsqrt(jnp.mean(v * v, axis=1, keepdims=True) + epsilon)
        for b in range(blocks):
            lane = slice(b * 128, b * 128 + 128)
            n = (v[:, lane] * r * gain[b]).astype(jnp.bfloat16)
            normed_out[at, lane] = n
            x_out[pl.ds(i * step_rows * blocks + b, step_rows, stride=blocks), :] = n.astype(jnp.float32)

    damping = [jax.nn.sigmoid(par_out[j]) for j in range(dims)]
    keep = [1.0 - damping[j] * jax.nn.sigmoid(par_out[dims + j]) for j in range(dims)]
    weight = [damping[j] * par_out[2 * dims + j] * par_out[3 * dims + j] for j in range(dims)]
    omega = par_out[4 * dims + 1]

    def row(ref, p):
        return ref[pl.ds(pl.multiple_of(p * blocks, blocks), blocks), :]

    def first_pass(p, state):
        x, a = row(x_out, p), alive[pl.ds(p, 1), :]
        return tuple(keep[j] * (state[j] * a) + x for j in range(dims))

    zero = tuple(jnp.zeros((blocks, 128), jnp.float32) for _ in range(dims))
    pump()
    ends = zero
    for part in range(2):
        ends = lax.fori_loop(part * rows // 2, (part + 1) * rows // 2, first_pass, ends, unroll=4)
        if part == 0:
            pump()
    for j in range(dims):
        bound[s, j] = ends[j]
    out = []
    for d in range(1, nq):
        out.append(pltpu.make_async_remote_copy(
            bound.at[s], bound.at[s], sends_b.at[d - 1], recv_b.at[d - 1],
            device_id=seq_peer[d - 1], device_id_type=MESH))
        out[-1].start()
    pump(3)
    for d in range(1, nq):
        came = bound.at[lax.rem(s + nq - d, nq)]
        pltpu.make_async_remote_copy(
            came, came, sends_b.at[d - 1], recv_b.at[d - 1],
            device_id=seq_peer[d - 1], device_id_type=MESH).wait_recv()
    for j in range(dims):
        through = power(keep[j], rows)
        state = jnp.zeros((blocks, 128), jnp.float32)
        for e in range(nq - 1):
            later = through * spans[e : e + 1, :] * state + bound[e, j]
            state = jnp.where(e < s, later, state)
        carry_out[j] = state

    def second_pass(p, state):
        x, a = row(x_out, p), alive[pl.ds(p, 1), :]
        state = tuple(keep[j] * (state[j] * a) + x for j in range(dims))
        sums = [omega * x] + [weight[j] * state[j] for j in range(dims)]
        while len(sums) > 1:
            sums = [sum(sums[k : k + 2][1:], sums[k]) for k in range(0, len(sums), 2)]
        mixed_out[pl.ds(pl.multiple_of(p * blocks, blocks), blocks), :] = sums[0]
        return state

    state = tuple(carry_out[j] for j in range(dims))
    for part in range(4):
        state = lax.fori_loop(part * rows // 4, (part + 1) * rows // 4, second_pass, state, unroll=4)
        if part % 2:
            pump()
    for b in range(blocks):
        m = mixed_out[pl.ds(b, rows, stride=blocks), :]
        active_out[:, b * 128 : b * 128 + 128] = (m * jax.nn.sigmoid(m)).astype(jnp.bfloat16)
    for copy in copies + out:
        copy.wait_send()

    flushes = []

    def flush(ref, hbm):
        copy = pltpu.make_async_copy(ref, hbm, flush_sem.at[len(flushes)])
        copy.start()
        flushes.append(copy)

    def pieces(i):
        while i not in done:
            pump()

        def fetch(g):
            return pltpu.make_async_copy(
                wholes[i].at[g // grid.nc, g % grid.nc], slots[i].at[g % 2], load_sem.at[i, g % 2]
            )

        fetch(0).start()
        for g in range(grid.ng):
            if g + 1 < grid.ng:
                fetch(g + 1).start()
            fetch(g).wait()
            piece = slots[i][g % 2]
            wide = piece.shape[-1]
            yield g, slice(g * wide, g * wide + wide), piece.reshape(-1, wide)
            pump()

    block_rows = 32
    zdim = aff_out.shape[1]
    vdim = value_pre.shape[1]
    first_gate, first_reset, first_cand = width, width + zdim, width + zdim + vdim
    dot = functools.partial(jnp.dot, preferred_element_type=jnp.float32)

    def by_rows(count=rows, each=block_rows):
        def wrap(f):
            pl.loop(0, count // each)(lambda i: f(pl.ds(pl.multiple_of(i * each, each), each)))

        return wrap

    for g, cols, piece in pieces(0):
        proj[:, cols] = dot(active_out[...], piece)
    flush(proj, proj_hbm)

    scale_q = zdim**-0.5
    near = []
    for r in range(rows // STRETCH):
        at = slice(r * STRETCH, r * STRETCH + STRETCH)
        gate = proj[at, first_gate:first_reset]
        shared = gate * jax.nn.sigmoid(gate)
        query = (scale_q * (shared * aff_out[0:1] + aff_out[1:2])).astype(jnp.bfloat16)
        key = (shared * aff_out[2:3] + aff_out[3:4]).astype(jnp.bfloat16)
        scores = lax.dot_general(query, key, (((1,), (1,)), ((), ())), preferred_element_type=jnp.float32)
        scores = jnp.where(mask[at, :] > 0.0, scores, -1e30)
        expo = jnp.exp(scores - jnp.max(scores, axis=1, keepdims=True))
        probs = expo / jnp.sum(expo, axis=1, keepdims=True)
        probs_out[at, :] = probs
        near.append(probs.astype(jnp.bfloat16))

    for g, cols, piece in pieces(1):
        pre = dot(normed_out[...], piece)
        value_pre[:, cols] = pre
        values[:, cols] = (pre * jax.nn.sigmoid(pre)).astype(jnp.bfloat16)
    flush(value_pre, value_hbm)
    for r in range(rows // STRETCH):
        at = slice(r * STRETCH, r * STRETCH + STRETCH)
        att[at, :] = dot(near[r], values[at, :])

    @by_rows()
    def _(at):
        gate = proj[at, first_reset:first_cand]
        hin[at, :] = (att[at, :] * (gate * jax.nn.sigmoid(gate))).astype(jnp.bfloat16)

    flush(att, att_hbm)
    flush(hin, hin_hbm)

    for g, cols, piece in pieces(2):
        hpre[:, cols] = proj[:, first_cand + cols.start : first_cand + cols.stop] + dot(hin[...], piece)
    flush(hpre, hpre_hbm)

    gain_two = [par_out[4 * dims + 2, b : b + 1, :] for b in range(blocks)]

    @by_rows()
    def _(at):
        v = tok[at, :].astype(jnp.float32)
        h = hpre[at, :]
        one = v + jax.nn.sigmoid(proj[at, 0:width]) * (h * jax.nn.sigmoid(h) - v)
        out_one_out[at, :] = one
        r = lax.rsqrt(jnp.mean(one * one, axis=1, keepdims=True) + epsilon)
        for b in range(blocks):
            lane = slice(b * 128, b * 128 + 128)
            two_out[at, lane] = (one[:, lane] * r * gain_two[b]).astype(jnp.bfloat16)

    for g, cols, piece in pieces(3):
        pre = dot(two_out[...], piece)
        ffn_pre[:, cols] = pre
        act[:, cols] = (pre * jax.nn.sigmoid(pre)).astype(jnp.bfloat16)
    flush(ffn_pre, ffn_hbm)
    flush(act, act_hbm)
    for g, cols, piece in pieces(4):
        layer_out[:, cols] = (out_one_out[:, cols] + dot(act[...], piece)).astype(jnp.bfloat16)
    for _ in steps:
        pass
    for copy in flushes:
        copy.wait()


def power(v, n):
    result = None
    while n:
        if n & 1:
            result = v if result is None else result * v
        n >>= 1
        if n:
            v = v * v
    return result


def mix_forward(grid, weights, cuts, tok, tile, alive, spans, mask, dims, collective_id):
    rows, width = tok.shape
    nq, ng = grid.nq, grid.ng
    blocks = width // 128
    f = jnp.float32
    vm = pl.BlockSpec(memory_space=pltpu.VMEM)
    shapes, shards, outs, count = gather_plan(grid, weights, cuts)
    n = len(shards)
    vdim, fdim, proj_dim = weights[1].shape[1] * ng, weights[3].shape[1] * ng, weights[0].shape[1] * ng
    low = jnp.bfloat16
    kept = [
        ((rows, proj_dim), f),
        ((rows, vdim), f),
        ((rows, vdim), f),
        ((rows, vdim), low),
        ((rows, width), f),
        ((rows, fdim), f),
        ((rows, fdim), low),
    ]
    local = [
        ((rows, width), low),
        ((rows, width), low),
        ((rows * blocks, 128), f),
        ((rows * blocks, 128), f),
        ((dims, blocks, 128), f),
        ((4 * dims + 3, blocks, 128), f),
        ((4, 128), f),
        ((rows, STRETCH), f),
        ((rows, width), f),
        ((rows, width), low),
        ((rows, width), low),
    ]
    result = pl.pallas_call(
        functools.partial(mix_kernel, grid, width, dims, shapes),
        out_shape=outs + [jax.ShapeDtypeStruct(*v) for v in local + kept],
        in_specs=[ANY] * n + [vm] * 5,
        out_specs=[ANY] * n + [vm] * len(local) + [ANY] * len(kept),
        scratch_shapes=[pltpu.VMEM(*v) for v in kept]
        + [
            pltpu.VMEM((rows, vdim), low),
            pltpu.VMEM((ng - 1,) + tile.shape, f),
            pltpu.VMEM((nq,) + tile.shape, f),
            pltpu.VMEM((nq, dims, blocks, 128), f),
            pltpu.SemaphoreType.DMA((nq + ng - 2,)),
            pltpu.SemaphoreType.DMA((nq + ng - 2,)),
            pltpu.SemaphoreType.DMA((nq - 1,)),
            pltpu.SemaphoreType.DMA((nq - 1,)),
            pltpu.SemaphoreType.DMA((n,)),
            pltpu.SemaphoreType.DMA((len(kept),)),
            pltpu.SemaphoreType.DMA((n, 2)),
            pltpu.SemaphoreType.DMA((count,)),
            pltpu.SemaphoreType.DMA((count,)),
        ]
        + [pltpu.VMEM((2,) + o.shape[2:], o.dtype) for o in outs],
        compiler_params=pltpu.CompilerParams(
            collective_id=collective_id, has_side_effects=True, vmem_limit_bytes=60 << 20
        ),
    )(*shards, tok, tile, alive, spans, mask)
    return result[:n], result[n:]


def scan_back(grid, dims, g_rows, x_in, mixed, carry, par, alive, spans, gin_rows, before, bound, sends_b, recv_b,
              m_all, k_all, seq_peer, s, pump):
    nq = grid.nq
    blocks = carry.shape[1]
    rows = g_rows.shape[0] // blocks

    @pl.loop(0, rows * blocks // 64)
    def _(i):
        at = pl.ds(pl.multiple_of(i * 64, 64), 64)
        g_rows[at, :] = g_rows[at, :] * silu_slope(mixed[at, :])

    damping = [jax.nn.sigmoid(par[j]) for j in range(dims)]
    keep = [1.0 - damping[j] * jax.nn.sigmoid(par[dims + j]) for j in range(dims)]
    weight = [damping[j] * par[2 * dims + j] * par[3 * dims + j] for j in range(dims)]
    omega = par[4 * dims + 1]

    def row(ref, p):
        return ref[pl.ds(pl.multiple_of(p * blocks, blocks), blocks), :]

    def first_pass(i, flow):
        p = rows - 1 - i
        gp, a = row(g_rows, p), alive[pl.ds(p, 1), :]
        return tuple(keep[j] * (a * (gp + flow[j])) for j in range(dims))

    zero = jnp.zeros((blocks, 128), jnp.float32)
    ends = lax.fori_loop(0, rows, first_pass, (zero,) * dims, unroll=4)
    for j in range(dims):
        bound[s, j] = ends[j]
    def sent(d):
        return pltpu.make_async_remote_copy(
            bound.at[s], bound.at[s], sends_b.at[d - 1], recv_b.at[d - 1],
            device_id=seq_peer[d - 1], device_id_type=MESH)

    for d in range(1, nq):
        sent(d).start()
    pump()
    for d in range(1, nq):
        came = bound.at[lax.rem(s + nq - d, nq)]
        pltpu.make_async_remote_copy(
            came, came, sends_b.at[d - 1], recv_b.at[d - 1],
            device_id=seq_peer[d - 1], device_id_type=MESH).wait_recv()
    flow_in = []
    for j in range(dims):
        through = power(keep[j], rows)
        flow = zero
        for e in range(nq - 1, 0, -1):
            later = through * spans[e : e + 1, :] * flow + bound[e, j]
            flow = jnp.where(e > s, later, flow)
        flow_in.append(flow)

    few = before.shape[1]
    for j0 in range(0, dims, few):
        js = range(j0, j0 + few)

        def ahead(p, state):
            x, a = row(x_in, p), alive[pl.ds(p, 1), :]
            for t in range(few):
                before[p, t] = state[t]
            return tuple(keep[j] * (state[t] * a) + x for t, j in enumerate(js))

        lax.fori_loop(0, rows, ahead, tuple(carry[j] for j in js), unroll=4)
        if j0:
            pump()

        def back(i, held):
            flow, m_sum, k_sum, om_sum = held
            p = rows - 1 - i
            at = pl.ds(pl.multiple_of(p * blocks, blocks), blocks)
            gp, x, a = g_rows[at, :], x_in[at, :], alive[pl.ds(p, 1), :]
            total = omega * gp if j0 == 0 else gin_rows[at, :]
            if j0 == 0:
                om_sum = om_sum + gp * x
            new_flow, new_m, new_k = [], [], []
            for t, j in enumerate(js):
                c = gp + flow[t]
                ac = a * c
                total = total + weight[j] * c
                new_flow.append(keep[j] * ac)
                new_m.append(m_sum[t] + c * x)
                new_k.append(k_sum[t] + ac * before[p, t])
            gin_rows[at, :] = total
            return tuple(new_flow), tuple(new_m), tuple(new_k), om_sum

        zeros = (zero,) * few
        _, m_sum, k_sum, om_sum = lax.fori_loop(
            0, rows, back, (tuple(flow_in[j] for j in js), zeros, zeros, zero), unroll=4
        )
        for t, j in enumerate(js):
            m_all[j] = m_sum[t]
            k_all[j] = k_sum[t]
        if j0 == 0:
            m_all[dims] = om_sum
        pump()
    for d in range(1, nq):
        sent(d).wait_send()


def norm_back(par, dims, tok, pre, direct, gin_rows, gtok_out, row_sums):
    rows, width = tok.shape
    blocks = width // 128
    gain = [par[4 * dims, b : b + 1, :] for b in range(blocks)]
    lanes = [slice(b * 128, b * 128 + 128) for b in range(blocks)]
    step_rows = 32

    def some(i, gains):
        at = pl.ds(pl.multiple_of(i * step_rows, step_rows), step_rows)
        v = tok[at, :].astype(jnp.float32)
        r = lax.rsqrt(jnp.mean(v * v, axis=1, keepdims=True) + epsilon)
        gy = []
        for b in range(blocks):
            came = gin_rows[pl.ds(i * step_rows * blocks + b, step_rows, stride=blocks), :]
            gy.append(pre[at, lanes[b]] + came.astype(jnp.bfloat16).astype(jnp.float32))
        scaled = [gy[b] * gain[b] for b in range(blocks)]
        dots = sum(jnp.sum(scaled[b] * v[:, lanes[b]], axis=1, keepdims=True) for b in range(blocks))
        pull = r * r * (dots / width)
        new = []
        for b in range(blocks):
            vb = v[:, lanes[b]]
            gx = r * (scaled[b] - vb * pull)
            gtok_out[at, lanes[b]] = (direct[at, lanes[b]] + gx).astype(jnp.bfloat16)
            new.append(gains[b] + jnp.sum(gy[b] * (vb * r), axis=0, keepdims=True))
        return tuple(new)

    gains = lax.fori_loop(
        0, rows // step_rows, some, tuple(jnp.zeros((1, 128), jnp.float32) for _ in range(blocks))
    )
    for b in range(blocks):
        row_sums[b : b + 1, :] = gains[b]


def fill_small(grid, dims, small, m_all, k_all, row_sums):
    blocks = row_sums.shape[0]
    for e in range(grid.nq):
        b = block_of(e, grid.nq, blocks)
        small[e, 0:dims] = m_all[0:dims, b, :]
        small[e, dims : 2 * dims] = k_all[:, b, :]
        small[e, 2 * dims : 2 * dims + 1] = m_all[dims, b : b + 1, :]
        small[e, 2 * dims + 1 : 2 * dims + 2] = row_sums[b : b + 1, :]


def mix_back_kernel(grid, dims, shapes, *refs):
    n = len(shapes)
    terms, refs = refs[:n], refs[n:]
    gact, x_in, mixed, carry, par, alive, spans, tok, pre, direct, small_in, *refs = refs
    sums, refs = refs[:n], refs[n:]
    (gtok_out, small_out,
     g_rows, gin_rows, before, bound, m_all, k_all, row_sums, small, seq_in, seg_in,
     sends_b, recv_b, s_send, s_recv, own_sem, send, recv, *scratch) = refs
    nq = grid.nq
    rows, width = gact.shape
    blocks = width // 128
    s = lax.axis_index("seq")
    seq_peer, seg_peer = small_peers(grid)
    meet(seq_peer + seg_peer)
    steps = scatter_steps(grid, shapes, terms, sums, scratch, own_sem, Sems(send, recv))
    little = SmallSum(grid, small, small_out, seq_in, seg_in, s_send, s_recv)

    def pump(count=1):
        for _ in range(count):
            next(steps, None)

    pump(2)
    for b in range(blocks):
        g_rows[pl.ds(b, rows, stride=blocks), :] = gact[:, b * 128 : b * 128 + 128].astype(jnp.float32)

    scan_back(
        grid, dims, g_rows, x_in, mixed, carry, par, alive, spans, gin_rows, before, bound, sends_b, recv_b,
        m_all, k_all, seq_peer, s, pump
    )
    norm_back(par, dims, tok, pre, direct, gin_rows, gtok_out, row_sums)
    for e in range(nq):
        small[e] = small_in[e]
    fill_small(grid, dims, small, m_all, k_all, row_sums)
    little.start()
    pump()
    little.middle()
    for _ in steps:
        pass
    little.end()


def mix_backward(grid, terms, cuts, gact, x_in, mixed, carry, par, alive, spans, tok, pre, direct, small, collective_id):
    rows, width = gact.shape
    nq, ng = grid.nq, grid.ng
    blocks, dims, few = width // 128, carry.shape[0], 4
    f = jnp.float32
    vm = pl.BlockSpec(memory_space=pltpu.VMEM)
    shapes, outs, scratch, count = scatter_plan(grid, terms, cuts)
    parts = [t.reshape((grid.ny, grid.nc, grid.nz, grid.nx) + v) for t, v in zip(terms, shapes)]
    n = len(parts)
    result = pl.pallas_call(
        functools.partial(mix_back_kernel, grid, dims, shapes),
        out_shape=outs
        + [jax.ShapeDtypeStruct((rows, width), jnp.bfloat16), jax.ShapeDtypeStruct(small.shape[1:], f)],
        in_specs=[ANY] * n + [vm] * 11,
        out_specs=[vm] * (n + 2),
        scratch_shapes=[
            pltpu.VMEM((rows * blocks, 128), f),
            pltpu.VMEM((rows * blocks, 128), f),
            pltpu.VMEM((rows, few, blocks, 128), f),
            pltpu.VMEM((nq, dims, blocks, 128), f),
            pltpu.VMEM((dims + 1, blocks, 128), f),
            pltpu.VMEM((dims, blocks, 128), f),
            pltpu.VMEM((blocks, 128), f),
            pltpu.VMEM(small.shape, f),
            pltpu.VMEM((nq - 1,) + small.shape[1:], f),
            pltpu.VMEM((ng - 1,) + small.shape[1:], f),
            pltpu.SemaphoreType.DMA((nq - 1,)),
            pltpu.SemaphoreType.DMA((nq - 1,)),
            pltpu.SemaphoreType.DMA((nq + ng - 2,)),
            pltpu.SemaphoreType.DMA((nq + ng - 2,)),
            pltpu.SemaphoreType.DMA((n, 2)),
            pltpu.SemaphoreType.DMA((count,)),
            pltpu.SemaphoreType.DMA((count,)),
        ]
        + scratch,
        compiler_params=pltpu.CompilerParams(
            collective_id=collective_id, has_side_effects=True, vmem_limit_bytes=62 << 20
        ),
    )(*parts, gact, x_in, mixed, carry, par, alive, spans, tok, pre, direct, small)
    return [v.reshape(-1, t.shape[-1]) for v, t in zip(result, terms)], result[n], result[n + 1]


def layer_back_kernel(grid, dims, shapes, sizes, *refs):
    n = len(shapes)
    zdim, vdim, fdim = sizes
    wholes, refs = refs[:n], refs[n:]
    (cot_hbm, act_hbm, ffn_hbm, two_hbm, one_hbm, hpre_hbm, proj_hbm, att_hbm, hin_hbm, value_hbm, probs, active_hbm,
     normed_hbm, tok_hbm, x_hbm, mixed_hbm, carry, par, aff, alive, spans, *refs) = refs
    sums, refs = refs[:n], refs[n:]
    gtok_out, small_out, *refs = refs
    terms, refs = refs[:n], refs[n:]
    (gproj, direct, pre, bound, m_all, k_all, row_sums, two_sums, aff_sums, small, seq_in, seg_in,
     sends_b, recv_b, s_send, s_recv, own_sem, load_sem, tile_sem, stage_sem, send, recv, *scratch) = refs
    nq, ng, nc, nz = grid.nq, grid.ng, grid.nc, grid.nz
    rows, width = direct.shape
    blocks = width // 128
    low, f = jnp.bfloat16, jnp.float32
    s = lax.axis_index("seq")
    seq_peer, seg_peer = small_peers(grid)
    meet(seq_peer + seg_peer)
    ready = [0]
    steps = scatter_steps(grid, shapes, terms, sums, scratch, own_sem, Sems(send, recv), lambda: ready[0])
    little = SmallSum(grid, small, small_out, seq_in, seg_in, s_send, s_recv)
    loads = [0]

    def pump(count=1):
        for _ in range(count):
            next(steps, None)

    pump()
    dot = functools.partial(jnp.dot, preferred_element_type=f)

    def dot_nt(a, b):
        return lax.dot_general(a, b, (((1,), (1,)), ((), ())), preferred_element_type=f)

    def dot_tn(a, b):
        return lax.dot_general(a, b, (((0,), (0,)), ((), ())), preferred_element_type=f)

    def fetch(src, dst):
        copy = pltpu.make_async_copy(src, dst, load_sem.at[loads[0]])
        loads[0] += 1
        copy.start()
        return copy.wait

    def by_rows(each=32):
        def wrap(some):
            pl.loop(0, rows // each)(lambda i: some(pl.ds(pl.multiple_of(i * each, each), each)))

        return wrap

    def wide(i):
        return shapes[i][-1]

    def tile_shape(i):
        return (2, grid.ny, nc, grid.nx) + shapes[i]

    def depth(i):
        return grid.nx * shapes[i][0] * shapes[i][1]

    def tile(i, tiles, zt):
        return pltpu.make_async_copy(wholes[i].at[:, :, zt], tiles.at[zt % 2], tile_sem.at[zt % 2])

    def begin(i, tiles):
        for zt in range(min(2, nz)):
            tile(i, tiles, zt).start()

    def against(i, tiles, part):
        for zt in range(nz):
            tile(i, tiles, zt).wait()
            total = None
            for g in range(ng):
                term = dot_nt(part(g), tiles[zt % 2, g // nc, g % nc].reshape(depth(i), wide(i)))
                total = term if total is None else total + term
            if zt + 2 < nz:
                tile(i, tiles, zt + 2).start()
            if zt == 1:
                pump()
            yield slice(zt * depth(i), zt * depth(i) + depth(i)), total

    def grads(i, left, stage, part):
        copies = []
        slots = stage.shape[0]
        for g in range(ng):
            right = part(g)
            for zt in range(nz):
                k = len(copies)
                if k >= slots:
                    copies[k - slots].wait()
                d = depth(i)
                term = dot(left[zt * d : zt * d + d, :], right)
                stage[k % slots] = term.astype(low).reshape(stage.shape[1:])
                copies.append(
                    pltpu.make_async_copy(stage.at[k % slots], terms[i].at[g // nc, g % nc, zt], stage_sem.at[k % slots])
                )
                copies[k].start()
        for copy in copies[-slots:]:
            copy.wait()
        ready[0] = i + 1

    def turned(src, dst):
        for a in range(0, src.shape[1], 256):
            b = min(a + 256, src.shape[1])
            dst[a:b, :] = src[:, a:b].T

    def vm(*shape, kind=low):
        return pltpu.VMEM(shape, kind)

    def stage_of(i, slots=4):
        return pltpu.VMEM((slots, grid.nx) + shapes[i], low)

    def cut(ref, i):
        return lambda g: ref[:, g * wide(i) : (g + 1) * wide(i)]

    first_gate, first_reset, first_cand = width, width + zdim, width + zdim + vdim
    out_i, in_i, att_i, value_i, mix_i = range(5)

    def ffn_back(cot, hold, norm_grad, two):
        wait_cot, wait_act, wait_two = fetch(cot_hbm, cot), fetch(act_hbm, hold), fetch(two_hbm, two)

        def second(pre_act, left, stage, tiles):
            begin(out_i, tiles)
            each = depth(out_i)
            pre_waits = [fetch(ffn_hbm.at[:, k * each : (k + 1) * each], pre_act.at[k]) for k in range(2)]
            wait_act()
            turned(hold, left)
            wait_cot()
            grads(out_i, left, stage, cut(cot, out_i))
            pump()
            for k, (cols, grad) in enumerate(against(out_i, tiles, cut(cot, out_i))):
                pre_waits[k]()
                hold[:, cols] = (grad * silu_slope(pre_act[k % 2])).astype(low)
                if k + 2 < nz:
                    pre_waits.append(fetch(ffn_hbm.at[:, (k + 2) * each : (k + 3) * each], pre_act.at[k % 2]))
            pump()

        pl.run_scoped(
            second, vm(2, rows, depth(out_i), kind=f), vm(fdim, rows), stage_of(out_i), pltpu.VMEM(tile_shape(out_i), low)
        )

        def rest(one, hpre, upd, tok):
            waits = [fetch(one_hbm, one), fetch(hpre_hbm, hpre), fetch(proj_hbm.at[:, 0:width], upd), fetch(tok_hbm, tok)]

            def first(left, stage, tiles):
                begin(in_i, tiles)
                wait_two()
                turned(two, left)
                grads(in_i, left, stage, cut(hold, in_i))
                pump()
                for cols, grad in against(in_i, tiles, cut(hold, in_i)):
                    norm_grad[:, cols] = grad

            pl.run_scoped(first, vm(width, rows), stage_of(in_i), pltpu.VMEM(tile_shape(in_i), low))
            for wait in waits:
                wait()
            two_sums[...] = jnp.zeros_like(two_sums)

            @by_rows(16)
            def _(at):
                v, x, h, c = one[at, :], tok[at, :].astype(f), hpre[at, :], cot[at, :].astype(f)
                gain = jnp.concatenate([par[4 * dims + 2, b : b + 1, :] for b in range(blocks)], axis=1)
                r = lax.rsqrt(jnp.mean(v * v, axis=1, keepdims=True) + epsilon)
                gy = norm_grad[at, :]
                scaled = gy * gain
                pull = r * r * jnp.mean(scaled * v, axis=1, keepdims=True)
                grad_one = c + r * (scaled - v * pull)
                two_sums[...] += jnp.sum(gy * (v * r), axis=0, keepdims=True)
                u = jax.nn.sigmoid(upd[at, :])
                sig = jax.nn.sigmoid(h)
                direct[at, :] = grad_one * (1.0 - u)
                gproj[at, first_cand:] = (grad_one * u * (sig * (1.0 + h * (1.0 - sig)))).astype(low)
                gproj[at, 0:width] = (grad_one * (h * sig - x) * (u * (1.0 - u))).astype(low)

        pl.run_scoped(
            rest, vm(rows, width, kind=f), vm(rows, width, kind=f), vm(rows, width, kind=f), vm(rows, width)
        )

    pl.run_scoped(ffn_back, vm(rows, width), vm(rows, fdim), vm(rows, width, kind=f), vm(rows, width))
    pump()

    def attention_back(grad_hin, att, gate, shared_pre, value_pre):
        waits = [
            fetch(att_hbm, att),
            fetch(proj_hbm.at[:, first_reset:first_cand], gate),
            fetch(proj_hbm.at[:, first_gate:first_reset], shared_pre),
            fetch(value_hbm, value_pre),
        ]

        def out_back(hin, left, stage, tiles):
            wait_hin = fetch(hin_hbm, hin)
            begin(att_i, tiles)
            wait_hin()
            turned(hin, left)

            def part(g):
                return gproj[:, first_cand + g * wide(att_i) : first_cand + (g + 1) * wide(att_i)]

            grads(att_i, left, stage, part)
            pump()
            for cols, grad in against(att_i, tiles, part):
                grad_hin[:, cols] = grad

        pl.run_scoped(out_back, vm(rows, vdim), vm(vdim, rows), stage_of(att_i), pltpu.VMEM(tile_shape(att_i), low))

        def inner(grad_pre, normed, value_tiles):
            wait_normed = fetch(normed_hbm, normed)
            begin(value_i, value_tiles)

            def blocks_back(grad_att, values):
                for wait in waits:
                    wait()

                @by_rows(16)
                def _(at):
                    v, g, p = gate[at, :], grad_hin[at, :], value_pre[at, :]
                    sig = jax.nn.sigmoid(v)
                    grad_att[at, :] = (g * (v * sig)).astype(low)
                    gproj[at, first_reset:first_cand] = (g * att[at, :] * (sig * (1.0 + v * (1.0 - sig)))).astype(low)
                    values[at, :] = (p * jax.nn.sigmoid(p)).astype(low)

                aff_total = [jnp.zeros((1, zdim), f)] * 4
                scale_q = zdim**-0.5
                for r in range(rows // STRETCH):
                    at = slice(r * STRETCH, r * STRETCH + STRETCH)
                    v = shared_pre[at, :]
                    shared = v * jax.nn.sigmoid(v)
                    query = (scale_q * (shared * aff[0:1] + aff[1:2])).astype(low)
                    key = (shared * aff[2:3] + aff[3:4]).astype(low)
                    prob, ga = probs[at, :], grad_att[at, :]
                    grad_prob = dot_nt(ga, values[at, :])
                    weighted = jnp.sum(prob * grad_prob, axis=1, keepdims=True)
                    grad_score = (prob * (grad_prob - weighted)).astype(low)
                    grad_query = dot(grad_score, key) * scale_q
                    grad_key = dot_tn(grad_score, query)
                    grad_shared = grad_query * aff[0:1] + grad_key * aff[2:3]
                    gproj[at, first_gate:first_reset] = (grad_shared * silu_slope(v)).astype(low)
                    for k, t in enumerate([grad_query * shared, grad_query, grad_key * shared, grad_key]):
                        aff_total[k] = aff_total[k] + jnp.sum(t, axis=0, keepdims=True)
                    grad_hin[at, :] = dot_tn(prob.astype(low), ga)
                for k in range(4):
                    aff_sums[k : k + 1, :] = aff_total[k]

                @by_rows(16)
                def _(at):
                    grad_pre[at, :] = (grad_hin[at, :] * silu_slope(value_pre[at, :])).astype(low)

            pl.run_scoped(blocks_back, vm(rows, vdim), vm(rows, vdim))
            pump()

            def value_back(left, stage):
                wait_normed()
                turned(normed, left)
                grads(value_i, left, stage, cut(grad_pre, value_i))
                for cols, grad in against(value_i, value_tiles, cut(grad_pre, value_i)):
                    pre[:, cols] = grad

            pl.run_scoped(value_back, vm(width, rows), stage_of(value_i))

        pl.run_scoped(inner, vm(rows, vdim), vm(rows, width), pltpu.VMEM(tile_shape(value_i), low))

    pl.run_scoped(
        attention_back, vm(rows, vdim, kind=f), vm(rows, vdim, kind=f), vm(rows, vdim, kind=f), vm(rows, zdim, kind=f),
        vm(rows, vdim, kind=f)
    )
    pump()

    def mix_back(g_rows, gin_rows, x_in, mixed, tok):
        waits = [fetch(x_hbm, x_in), fetch(mixed_hbm, mixed), fetch(tok_hbm, tok)]

        def mix_weight_back(active, left, stage, tiles):
            wait_active = fetch(active_hbm, active)
            begin(mix_i, tiles)
            wait_active()
            turned(active, left)
            grads(mix_i, left, stage, cut(gproj, mix_i))
            pump()
            for cols, grad in against(mix_i, tiles, cut(gproj, mix_i)):
                grad = grad.astype(low).astype(f)
                for b in range(cols.start // 128, cols.stop // 128):
                    lane = b * 128 - cols.start
                    g_rows[pl.ds(b, rows, stride=blocks), :] = grad[:, lane : lane + 128]

        pl.run_scoped(
            mix_weight_back, vm(rows, width), vm(width, rows), stage_of(mix_i), pltpu.VMEM(tile_shape(mix_i), low)
        )

        for wait in waits:
            wait()

        def scan(before):
            scan_back(
                grid, dims, g_rows, x_in, mixed, carry, par, alive, spans, gin_rows, before, bound, sends_b, recv_b,
                m_all, k_all, seq_peer, s, pump
            )

        pl.run_scoped(scan, vm(rows, 4, blocks, 128, kind=f))
        norm_back(par, dims, tok, pre, direct, gin_rows, gtok_out, row_sums)

    pl.run_scoped(
        mix_back, vm(rows * blocks, 128, kind=f), vm(rows * blocks, 128, kind=f), vm(rows * blocks, 128, kind=f),
        vm(rows * blocks, 128, kind=f), vm(rows, width)
    )
    small[...] = jnp.zeros_like(small)
    fill_small(grid, dims, small, m_all, k_all, row_sums)
    for e in range(nq):
        b = block_of(e, nq, blocks)
        small[e, 2 * dims + 2 : 2 * dims + 3] = two_sums[:, b * 128 : b * 128 + 128]
        small[e, 2 * dims + 3 : 2 * dims + 7] = aff_sums[...]
    little.start()
    pump()
    little.middle()
    for _ in steps:
        pass
    little.end()


def layer_backward(grid, wholes, cuts, kept, probs, carry, par, aff, alive, spans, sizes, collective_id):
    nq, ng = grid.nq, grid.ng
    dims, blocks = carry.shape[0], carry.shape[1]
    zdim, vdim, fdim = sizes
    width = blocks * 128
    rows = probs.shape[0]
    f = jnp.float32
    vm = pl.BlockSpec(memory_space=pltpu.VMEM)
    n = len(wholes)
    like = [jax.ShapeDtypeStruct((ng, w.size // ng // w.shape[-1], w.shape[-1]), w.dtype) for w in wholes]
    shapes, outs, scratch, count = scatter_plan(grid, like, cuts)
    whole_shapes = [jax.ShapeDtypeStruct(w.shape[:4] + s, w.dtype) for w, s in zip(wholes, shapes)]
    low = [w.reshape(v.shape) for w, v in zip(wholes, whole_shapes)]
    small_shape = (-(-(2 * dims + 7) // 8) * 8, 128)
    result = pl.pallas_call(
        functools.partial(layer_back_kernel, grid, dims, shapes, sizes),
        out_shape=outs
        + [jax.ShapeDtypeStruct((rows, width), jnp.bfloat16), jax.ShapeDtypeStruct(small_shape, f)]
        + whole_shapes,
        in_specs=[ANY] * n + [ANY] * 10 + [vm] + [ANY] * 5 + [vm] * 5,
        out_specs=[vm] * (n + 2) + [ANY] * n,
        scratch_shapes=[
            pltpu.VMEM((rows, width * 2 + zdim + vdim), jnp.bfloat16),
            pltpu.VMEM((rows, width), f),
            pltpu.VMEM((rows, width), f),
            pltpu.VMEM((nq, dims, blocks, 128), f),
            pltpu.VMEM((dims + 1, blocks, 128), f),
            pltpu.VMEM((dims, blocks, 128), f),
            pltpu.VMEM((blocks, 128), f),
            pltpu.VMEM((1, width), f),
            pltpu.VMEM((4, zdim), f),
            pltpu.VMEM((nq,) + small_shape, f),
            pltpu.VMEM((nq - 1,) + small_shape, f),
            pltpu.VMEM((ng - 1,) + small_shape, f),
            pltpu.SemaphoreType.DMA((nq - 1,)),
            pltpu.SemaphoreType.DMA((nq - 1,)),
            pltpu.SemaphoreType.DMA((nq + ng - 2,)),
            pltpu.SemaphoreType.DMA((nq + ng - 2,)),
            pltpu.SemaphoreType.DMA((n, 2)),
            pltpu.SemaphoreType.DMA((24,)),
            pltpu.SemaphoreType.DMA((2,)),
            pltpu.SemaphoreType.DMA((4,)),
            pltpu.SemaphoreType.DMA((count,)),
            pltpu.SemaphoreType.DMA((count,)),
        ]
        + scratch,
        compiler_params=pltpu.CompilerParams(
            collective_id=collective_id, has_side_effects=True, vmem_limit_bytes=63 << 20
        ),
    )(*low, *kept[:10], probs, *kept[10:], carry, par, aff, alive, spans)
    return [v.reshape(-1, t.shape[-1]) for v, t in zip(result, like)], result[n], result[n + 1]


def rms_forward(values, gain):
    inverse = lax.rsqrt(jnp.mean(values * values, axis=-1, keepdims=True) + epsilon)
    return (values * inverse * gain, inverse)


def rms_backward(grad_out, values, inverse, gain):
    scaled = grad_out * gain
    projection = jnp.mean(scaled * values, axis=-1, keepdims=True)
    grad_in = inverse * (scaled - values * inverse * inverse * projection)
    return (grad_in, jnp.sum(grad_out * values * inverse, axis=0))


def silu_slope(values):
    sigma_v = jax.nn.sigmoid(values)
    return sigma_v * (1.0 + values * (1.0 - sigma_v))


def times(left, pieces):
    return jnp.concatenate(
        [jnp.dot(left, pieces[i], preferred_element_type=jnp.float32) for i in range(pieces.shape[0])], axis=1
    )


def against(left, pieces):
    n = pieces.shape[2]
    return sum(
        lax.dot_general(
            left[:, i * n : i * n + n], pieces[i], (((1,), (1,)), ((), ())), preferred_element_type=jnp.float32
        )
        for i in range(pieces.shape[0])
    )


def over_rows(left, right, count):
    n = right.shape[1] // count
    return jnp.stack(
        [
            lax.dot_general(
                left, right[:, i * n : i * n + n], (((0,), (0,)), ((), ())), preferred_element_type=jnp.float32
            ).astype(jnp.bfloat16)
            for i in range(count)
        ]
    )


def masked_scores(query_blk, key_blk, allowed):
    raw_scores = jnp.einsum("cid,cjd->cij", query_blk, key_blk, preferred_element_type=jnp.float32)
    return jnp.where(allowed, raw_scores, -1e30)


def backward_apart(grid, cotangent, tokens_low, forward, weights, alive, spans, sizes):
    (normed_b, active, x_rows, mixed_rows, carry, par, affine, probs, out_one, normed_two_b, _,
     projected, value_pre, attended, hidden_in, hidden_pre, ffn_hidden, ffn_act) = forward
    ffn_hidden = ffn_hidden.astype(jnp.float32)
    token_count, model_width = tokens_low.shape
    nq, ng = grid.nq, grid.ng
    dims, blocks = carry.shape[0], carry.shape[1]
    zdim, vdim, _ = sizes
    block_count = token_count // STRETCH
    tokens_flat = tokens_low.astype(jnp.float32)
    mix_full, value_full, out_full, ffn_in_full, ffn_out_full = (w.reshape(ng, -1, w.shape[-1]) for w in weights)
    gain_two = par[4 * dims + 2].reshape(-1)
    update = jax.nn.sigmoid(projected[:, :model_width])
    gate_pre = projected[:, model_width : model_width + zdim + vdim]
    gate_rows = jax.nn.silu(gate_pre)
    shared = gate_rows[:, :zdim]
    reset_gate = gate_rows[:, zdim:]
    values_b = jax.nn.silu(value_pre).astype(jnp.bfloat16)
    scale_q = zdim ** (-0.5)
    query_b = (scale_q * (shared * affine[0] + affine[1])).astype(jnp.bfloat16)
    key_b = (shared * affine[2] + affine[3]).astype(jnp.bfloat16)
    query_blk = query_b.reshape(block_count, STRETCH, zdim)
    key_blk = key_b.reshape(block_count, STRETCH, zdim)
    value_blk = values_b.reshape(block_count, STRETCH, vdim)
    probs = probs.reshape(block_count, STRETCH, STRETCH)
    probs_b = probs.astype(jnp.bfloat16)
    hidden_act = jax.nn.silu(hidden_pre)
    inverse_two = lax.rsqrt(jnp.mean(out_one * out_one, axis=-1, keepdims=True) + epsilon)

    grad_y_b = cotangent
    grad_ffn_out = over_rows(ffn_act, grad_y_b, ng)
    grad_act = against(grad_y_b, ffn_out_full)
    grad_hidden_b = (grad_act * silu_slope(ffn_hidden)).astype(jnp.bfloat16)
    grad_ffn_in = over_rows(normed_two_b, grad_hidden_b, ng)
    grad_normed_two = against(grad_hidden_b, ffn_in_full)
    grad_norm_two, grad_gain_two = rms_backward(grad_normed_two, out_one, inverse_two, gain_two)
    grad_out_one = grad_y_b.astype(jnp.float32) + grad_norm_two
    grad_update = grad_out_one * (hidden_act - tokens_flat)
    grad_tokens_flat = grad_out_one * (1.0 - update)
    grad_hpre_b = (grad_out_one * update * silu_slope(hidden_pre)).astype(jnp.bfloat16)
    grad_out_weight = over_rows(hidden_in, grad_hpre_b, ng)
    grad_hidden_in = against(grad_hpre_b, out_full)
    grad_att_b = (grad_hidden_in * reset_gate).astype(jnp.bfloat16)
    grad_reset = grad_hidden_in * attended
    grad_att_blk = grad_att_b.reshape(block_count, STRETCH, vdim)
    grad_probs = jnp.einsum("civ,cjv->cij", grad_att_blk, value_blk, preferred_element_type=jnp.float32)
    weighted = jnp.sum(probs * grad_probs, axis=2, keepdims=True)
    grad_scores_b = (probs * (grad_probs - weighted)).astype(jnp.bfloat16)
    grad_query = jnp.einsum("cij,cjd->cid", grad_scores_b, key_blk, preferred_element_type=jnp.float32).reshape(
        token_count, zdim
    )
    grad_key = jnp.einsum("cij,cid->cjd", grad_scores_b, query_blk, preferred_element_type=jnp.float32).reshape(
        token_count, zdim
    )
    grad_values = jnp.einsum("cij,civ->cjv", probs_b, grad_att_blk, preferred_element_type=jnp.float32).reshape(
        token_count, vdim
    )
    grad_qs = grad_query * scale_q
    grad_shared = grad_qs * affine[0] + grad_key * affine[2]
    grad_affine = jnp.stack(
        [
            jnp.sum(grad_qs * shared, axis=0),
            jnp.sum(grad_qs, axis=0),
            jnp.sum(grad_key * shared, axis=0),
            jnp.sum(grad_key, axis=0),
        ]
    )
    grad_gate_pre = jnp.concatenate([grad_shared, grad_reset], axis=1) * silu_slope(gate_pre)
    grad_upre = grad_update * update * (1.0 - update)
    grad_proj_b = jnp.concatenate(
        [grad_upre.astype(jnp.bfloat16), grad_gate_pre.astype(jnp.bfloat16), grad_hpre_b], axis=1
    )
    grad_mix = over_rows(active, grad_proj_b, ng)
    grad_active_b = against(grad_proj_b, mix_full).astype(jnp.bfloat16)
    grad_vpre_b = (grad_values * silu_slope(value_pre)).astype(jnp.bfloat16)
    grad_value = over_rows(normed_b, grad_vpre_b, ng)
    grad_normed = against(grad_vpre_b, value_full)

    small = jnp.concatenate(
        [jnp.zeros((blocks, 2 * dims + 2, 128), jnp.float32), grad_gain_two.reshape(blocks, 1, 128)], axis=1
    )
    if nq != blocks:
        small = jnp.take(small, np.arange(nq) * blocks // nq, axis=0)
    small = jnp.concatenate([small, jnp.broadcast_to(grad_affine[None], (nq, 4, 128))], axis=1)
    small = jnp.pad(small, ((0, 0), (0, -small.shape[1] % 8), (0, 0)))
    return mix_backward(
        grid, [grad_ffn_out, grad_ffn_in, grad_out_weight, grad_value, grad_mix], SCATTER_CUTS, grad_active_b, x_rows,
        mixed_rows, carry, par, alive, spans, tokens_low, grad_normed, grad_tokens_flat, small, 1
    )


def body(
    tokens,
    starts,
    norm_gain,
    ema_delta,
    ema_alpha,
    ema_beta,
    ema_eta,
    ema_omega,
    mix_weight,
    value_weight,
    qk_affine,
    out_weight,
    ffn_gain,
    ffn_in,
    ffn_out,
    cotangent,
):
    seg_count, row_count, model_width = tokens.shape
    nq, ng = lax.axis_size("seq"), lax.axis_size("seg")
    grid = Grid(nq, ng)
    seq_index, seg_index = lax.axis_index("seq"), lax.axis_index("seg")
    seq_length = row_count * nq
    dims = ema_delta.shape[1]
    zdim = qk_affine.shape[0] * nq * ng // 4
    vdim = value_weight.shape[1] * ng
    token_count = seg_count * row_count
    blocks = model_width // 128

    index = seq_index * ng + seg_index
    mine = norm_gain.shape[0]
    columns = jnp.concatenate(
        [ema_delta.T, ema_alpha.T, ema_beta.T, ema_eta.T, norm_gain[None], ema_omega[None], ffn_gain[None]], axis=0
    ).astype(jnp.float32)
    count = columns.shape[0]
    tile = jnp.zeros((-(-(count + 4) // 8) * 8, 128), jnp.float32)
    tile = lax.dynamic_update_slice(tile, columns, (0, lax.rem(index * mine, 128)))
    part = qk_affine.shape[0]
    tile = lax.dynamic_update_slice(
        tile, qk_affine.astype(jnp.float32)[None], (count + index * part // 128, lax.rem(index * part, 128))
    )

    places = jnp.arange(seq_length, dtype=jnp.int32)
    goes_on = 1.0 - jnp.any(starts[0][None, :] == places[:, None], axis=1).astype(jnp.float32)
    spans = jnp.broadcast_to(jnp.min(goes_on.reshape(nq, row_count), axis=1)[:, None], (nq, 128))
    alive = lax.dynamic_slice_in_dim(goes_on, seq_index * row_count, row_count, 0)
    alive = jnp.broadcast_to(alive[:, None], (row_count, 128))

    positions_rows = seq_index * row_count + jnp.arange(row_count, dtype=jnp.int32)
    docs_rows = jnp.sum((starts[:, None, :] <= positions_rows[None, :, None]).astype(jnp.int32), axis=2)
    block_count = token_count // STRETCH
    block_docs = docs_rows.reshape(block_count, STRETCH)
    offsets = jnp.arange(STRETCH)
    allowed = (block_docs[:, :, None] == block_docs[:, None, :]) & (offsets[:, None] >= offsets[None, :])[None]
    mask = allowed.astype(jnp.float32).reshape(token_count, STRETCH)
    tokens_low = tokens.reshape(token_count, model_width)
    weights, forward = mix_forward(
        grid, [mix_weight, value_weight, out_weight, ffn_in, ffn_out], GATHER_CUTS, tokens_low, tile, alive, spans, mask, dims, 0
    )
    mix_full, value_full, out_full, ffn_in_full, ffn_out_full = weights
    (normed_b, active, x_rows, mixed_rows, carry, par, affine, probs, out_one, normed_two_b, result,
     projected, value_pre, attended, hidden_in, hidden_pre, ffn_hidden, ffn_act) = forward
    sizes = (zdim, vdim, ffn_act.shape[1])
    cotangent_low = cotangent.reshape(token_count, model_width)
    if min(w.shape[1] for w in (mix_weight, value_weight, out_weight, ffn_in, ffn_out)) < 128:
        result_back = backward_apart(grid, cotangent_low, tokens_low, forward, weights, alive, spans, sizes)
    else:
        kept = [cotangent_low, ffn_act, ffn_hidden, normed_two_b, out_one, hidden_pre, projected, attended, hidden_in,
                value_pre, active, normed_b, tokens_low, x_rows, mixed_rows]
        order = [weights[4], weights[3], weights[2], weights[1], weights[0]]
        result_back = layer_backward(
            grid, order, SCATTER_CUTS, kept, probs, carry, par, affine, alive, spans, sizes, 1
        )
    (g_ffn_out, g_ffn_in, g_out, g_value, g_mix), grad_tokens, sums = result_back
    return (
        result.reshape(seg_count, row_count, model_width),
        grad_tokens.reshape(seg_count, row_count, model_width),
        *small_outputs(sums, index, dims, ema_delta, ema_alpha, ema_beta, ema_eta, mine, part, g_mix, g_value, g_out, g_ffn_in, g_ffn_out),
    )


def small_outputs(sums, index, dims, ema_delta, ema_alpha, ema_beta, ema_eta, mine, part, g_mix, g_value, g_out, g_ffn_in, g_ffn_out):
    own = lax.dynamic_slice_in_dim(sums, lax.rem(index * mine, 128), mine, 1)
    m_sum, k_sum = own[:dims].T, own[dims : 2 * dims].T
    vectors = own[2 * dims : 2 * dims + 3]
    delta, alpha, beta, eta = (v.astype(jnp.float32) for v in (ema_delta, ema_alpha, ema_beta, ema_eta))
    damping, decay = jax.nn.sigmoid(delta), jax.nn.sigmoid(alpha)
    g_keep = damping * beta * eta * k_sum
    grad_eta = damping * beta * m_sum
    grad_beta = damping * eta * m_sum
    grad_alpha = -g_keep * damping * decay * (1.0 - decay)
    grad_delta = (beta * eta * m_sum - g_keep * decay) * damping * (1.0 - damping)
    grad_affine = lax.dynamic_slice(
        sums, (2 * dims + 3 + index * part // 128, lax.rem(index * part, 128)), (1, part)
    ).reshape(-1)
    return (vectors[1], grad_delta, grad_alpha, grad_beta, grad_eta, vectors[0],
            g_mix, g_value, grad_affine, g_out, vectors[2], g_ffn_in, g_ffn_out)


def solution(mesh):
    placed = (
        P("seg", "seq", None),
        P("seg", None),
        P(("seq", "seg")),
        P(("seq", "seg"), None),
        P(("seq", "seg"), None),
        P(("seq", "seg"), None),
        P(("seq", "seg"), None),
        P(("seq", "seg")),
        P("seq", "seg"),
        P("seq", "seg"),
        P(("seq", "seg")),
        P("seq", "seg"),
        P(("seq", "seg")),
        P("seq", "seg"),
        P("seq", "seg"),
        P("seg", "seq", None),
    )
    return jax.shard_map(
        body,
        mesh=mesh,
        in_specs=placed,
        out_specs=(P("seg", "seq", None),) * 2 + placed[2:15],
        check_vma=False,
    )
```

profile of v0, /device:TPU:0, one launch (start us, length us, event | category | flops | bytes accessed | tf_op | source)
XLA Modules:
  0.0 422.0 jit_solution(2392167747021810000)
XLA Ops:
  0.6 1.8 copy.43
  2.5 3.5 concatenate.3
  6.0 0.7 dynamic_update_slice.6
  6.7 0.7 bitcast_convert_fusion
  7.4 0.1 dynamic_update_slice.7.refs_6_
  7.5 0.0 copy-start.3
  7.5 0.8 fusion.2
  8.3 0.1 dynamic_slice.9
  8.3 0.8 broadcast_in_dim.42.refs_7_.refs_24_
  9.1 0.1 reduce_min.9
  9.2 0.7 broadcast_in_dim.43.refs_8_.refs_25_
  9.9 0.7 convert_reduce_fusion
  10.6 0.8 fusion.1.refs_9_
  11.4 0.0 copy-done.3
  11.4 202.1 %shard_map.271 = (bf16[2,2,4,2,8,16,1056]{6,5,4,3,2,1,0:T(8,128)(2,1)}, bf16[2,2,4,2,4,32,512]{6,5,4,3,2,1,0:T(8,128)(2,1)}, bf16[2,2,4,2,4,64,256]{6,5,4,3,2,1,...) custom-call(bf16[8,16,1056]{2,1,0:T(8,128)(2,1)} %bitcast.60, ...), custom_call_target="tpu_custom_call" | custom-call | tf_op jit(solution)/shard_map/pallas_call | solution.py:719
  213.5 0.0 copy-start.4
  213.6 0.0 copy-start.5
  213.6 0.0 copy-start.6
  213.6 0.0 copy-start.7
  213.6 0.0 copy-start
  213.6 194.2 %shard_map.272 = (f32[8,64,256]{2,1,0:T(8,128)}, f32[8,16,1024]{2,1,0:T(8,128)}, f32[4,64,256]{2,1,0:T(8,128)}, f32[4,32,512]{2,1,0:T(8,128)}, f32[8,16,1056]{2,...) custom-call(bf16[2,2,4,2,8,64,256]{6,5,4,3,2,1,0:T(8,128)(2,1)} %get, ...), custom_call_target="tpu_custom_call" | custom-call | tf_op jit(solution)/shard_map/pallas_call | solution.py:1298
  407.8 0.0 copy-start.2
  407.8 0.0 copy-start.1
  407.8 1.4 dynamic-slice_bitcast_fusion.2
  409.2 0.0 copy-done.4
  409.2 0.0 copy-done.5
  409.2 0.0 copy-done.6
  409.2 0.0 copy-done.7
  409.2 1.4 subtract_multiply_fusion
  410.6 2.1 copy.44
  412.7 1.3 dynamic-slice_bitcast_fusion.5
  414.0 0.0 copy-done
  414.0 0.8 copy.53
  414.8 1.9 copy.54
  416.6 1.7 copy.55
  418.3 1.7 copy.56
  420.0 0.0 copy-done.2
  420.0 0.8 copy.57
  420.8 0.0 copy-done.1
  420.8 0.8 copy.58
  (6 shorter events, 0.0 us)
Async XLA Ops:
  7.5 3.9 copy-start.3
  213.5 195.7 %copy-start.4 = (bf16[32,16]{0,1:T(8,128)(2,1)S(1)}, bf16[32,16]{0,1:T(8,128)(2,1)}, u32[]{:S(2)}) copy-start(bf16[32,16]{0,1:T(8,128)(2,1)} %param.19) | copy-start | bytes 3076
  213.6 195.6 %copy-start.5 = (bf16[32,16]{0,1:T(8,128)(2,1)S(1)}, bf16[32,16]{0,1:T(8,128)(2,1)}, u32[]{:S(2)}) copy-start(bf16[32,16]{0,1:T(8,128)(2,1)} %param.20) | copy-start | bytes 3076
  213.6 195.6 %copy-start.6 = (bf16[32,16]{0,1:T(8,128)(2,1)S(1)}, bf16[32,16]{0,1:T(8,128)(2,1)}, u32[]{:S(2)}) copy-start(bf16[32,16]{0,1:T(8,128)(2,1)} %param.21) | copy-start | bytes 3076
  213.6 195.6 %copy-start.7 = (bf16[32,16]{0,1:T(8,128)(2,1)S(1)}, bf16[32,16]{0,1:T(8,128)(2,1)}, u32[]{:S(2)}) copy-start(bf16[32,16]{0,1:T(8,128)(2,1)} %param.22) | copy-start | bytes 3076
  213.6 200.4 %copy-start = (bf16[256,1024]{1,0:T(8,128)(2,1)S(1)}, bf16[256,1024]{1,0:T(8,128)(2,1)}, u32[]{:S(2)}) copy-start(bf16[256,1024]{1,0:T(8,128)(2,1)} %get-tuple-element.45) | copy-start | bytes 1572868
  407.8 12.2 %copy-start.2 = (f32[8,16,1024]{2,1,0:T(8,128)S(1)}, f32[8,16,1024]{2,1,0:T(8,128)}, u32[]{:S(2)}) copy-start(f32[8,16,1024]{2,1,0:T(8,128)} %get-tuple-element.73) | copy-start | bytes 1572868
  407.8 13.0 %copy-start.1 = (f32[8,64,256]{2,1,0:T(8,128)S(1)}, f32[8,64,256]{2,1,0:T(8,128)}, u32[]{:S(2)}) copy-start(f32[8,64,256]{2,1,0:T(8,128)} %get-tuple-element.74) | copy-start | bytes 1572868
where the time goes:
time: 430 us; the launch traced here: 422 us
  Pallas kernels  396 us (92%)
  local copies, waits for them, and re-layouts  20 us (5%)
  other arithmetic  4.49 us (1%)
    pallas_call x1, Pallas kernels, mix_forward(): pl.pallas_call(functools.partial(mix_kernel, grid, width, dims, shapes),...  202 us
    pallas_call x1, Pallas kernels, layer_backward(): pl.pallas_call(functools.partial(layer_back_kernel, grid, dims, shapes, s...  194 us
    unnamed x24, local copies, waits for them, and re-layouts  11.5 us

commit v1 on v0

--- a/solution.py
+++ b/solution.py
@@ -432,16 +432,60 @@
     return e * blocks // nq
 
 
-def mix_kernel(grid, width, dims, shapes, *refs):
+def place_params(grid, own, tile, count, mine, part):
+    index = lax.axis_index("seq") * grid.ng + lax.axis_index("seg")
+    row = lax.broadcasted_iota(jnp.int32, (mine, 128), 0)
+    lane = lax.broadcasted_iota(jnp.int32, (mine, 128), 1)
+
+    def spread(first):
+        where = (lane == row + first).astype(jnp.bfloat16)
+        return lax.dot_general(own[...], where, (((0,), (0,)), ((), ())), preferred_element_type=jnp.float32)
+
+    tile[...] = jnp.zeros_like(tile)
+    tile[0:count, :] = spread(lax.rem(index * mine, 128))[0:count]
+    affine = spread(lax.rem(index * part, 128))[count : count + 1]
+    at = lax.broadcasted_iota(jnp.int32, (4, 128), 0) == index * part // 128
+    tile[count : count + 4, :] = jnp.where(at, affine, 0.0)
+
+
+def place_documents(grid, starts, alive, spans, mask):
+    rows = alive.shape[0]
+    first = [starts[0, k] for k in range(starts.shape[1])]
+    base = lax.axis_index("seq") * rows
+    place = lax.broadcasted_iota(jnp.int32, (rows, 128), 0)
+    column = lax.broadcasted_iota(jnp.int32, (rows, 128), 1)
+    within = jnp.bitwise_and(place, STRETCH - 1)
+    here, there = base + place, base + place - within + column
+    goes_on = jnp.ones((rows, 128), jnp.float32)
+    doc_here, doc_there = jnp.zeros((rows, 128), jnp.int32), jnp.zeros((rows, 128), jnp.int32)
+    for f in first:
+        goes_on = jnp.where(here == f, 0.0, goes_on)
+        doc_here = doc_here + jnp.where(here >= f, 1, 0)
+        doc_there = doc_there + jnp.where(there >= f, 1, 0)
+    alive[...] = goes_on
+    mask[...] = jnp.where((doc_here == doc_there) & (column <= within), 1.0, 0.0)
+    low = lax.broadcasted_iota(jnp.int32, spans.shape, 0) * rows
+    whole = jnp.ones(spans.shape, jnp.float32)
+    for f in first:
+        whole = jnp.where((low <= f) & (f < low + rows), 0.0, whole)
+    spans[...] = whole
+
+
+def mix_kernel(grid, width, dims, shapes, part, out_term, *refs):
     n = len(shapes)
     shards, refs = refs[:n], refs[n:]
-    tok, tile, alive, spans, mask, *refs = refs
+    tok, own_params, starts, cot, *refs = refs
     wholes, refs = refs[:n], refs[n:]
-    (normed_out, active_out, x_out, mixed_out, carry_out, par_out, aff_out, probs_out, out_one_out, two_out, layer_out,
-     proj_hbm, value_hbm, att_hbm, hin_hbm, hpre_hbm, ffn_hbm, act_hbm,
-     proj, value_pre, att, hin, hpre, ffn_pre, act, values,
-     tiles, table, bound, sends_t, recv_t, sends_b, recv_b, own_sem, flush_sem, load_sem, send, recv,
+    term_hbm = None
+    if out_term:
+        term_hbm, *refs = refs
+    (alive, spans, carry_out, par_out, aff_out, probs_out, layer_out,
+     normed_hbm, active_hbm, x_hbm, mixed_hbm, one_hbm, two_hbm, proj_hbm, value_hbm, att_hbm, hin_hbm, hpre_hbm, ffn_hbm, act_hbm,
+     normed_out, active_out, x_out, mixed_out, out_one_out, two_out, proj, value_pre, att, hin, hpre, ffn_pre, act, values,
+     mask, tile, tiles, table, bound, sends_t, recv_t, sends_b, recv_b, own_sem, flush_sem, load_sem, send, recv,
      *slots) = refs
+    if out_term:
+        *slots, turned_act, stage, stage_sem = slots
     nq, ng = grid.nq, grid.ng
     rows = tok.shape[0]
     blocks = width // 128
@@ -455,6 +499,16 @@
     def pump(count=1):
         for _ in range(count):
             done.update(next(steps, ()))
+
+    flushes = []
+
+    def flush(ref, hbm):
+        copy = pltpu.make_async_copy(ref, hbm, flush_sem.at[len(flushes)])
+        copy.start()
+        flushes.append(copy)
+
+    place_params(grid, own_params, tile, 4 * dims + 3, width // (nq * ng), part)
+    place_documents(grid, starts, alive, spans, mask)
 
     copies = []
     for d in range(1, ng):
@@ -507,6 +561,8 @@
             normed_out[at, lane] = n
             x_out[pl.ds(i * step_rows * blocks + b, step_rows, stride=blocks), :] = n.astype(jnp.float32)
 
+    flush(normed_out, normed_hbm)
+    flush(x_out, x_hbm)
     damping = [jax.nn.sigmoid(par_out[j]) for j in range(dims)]
     keep = [1.0 - damping[j] * jax.nn.sigmoid(par_out[dims + j]) for j in range(dims)]
     weight = [damping[j] * par_out[2 * dims + j] * par_out[3 * dims + j] for j in range(dims)]
@@ -565,15 +621,10 @@
     for b in range(blocks):
         m = mixed_out[pl.ds(b, rows, stride=blocks), :]
         active_out[:, b * 128 : b * 128 + 128] = (m * jax.nn.sigmoid(m)).astype(jnp.bfloat16)
+    flush(mixed_out, mixed_hbm)
+    flush(active_out, active_hbm)
     for copy in copies + out:
         copy.wait_send()
-
-    flushes = []
-
-    def flush(ref, hbm):
-        copy = pltpu.make_async_copy(ref, hbm, flush_sem.at[len(flushes)])
-        copy.start()
-        flushes.append(copy)
 
     def pieces(i):
         while i not in done:
@@ -592,7 +643,8 @@
             piece = slots[i][g % 2]
             wide = piece.shape[-1]
             yield g, slice(g * wide, g * wide + wide), piece.reshape(-1, wide)
-            pump()
+            if g + 1 == grid.ng:
+                pump()
 
     block_rows = 32
     zdim = aff_out.shape[1]
@@ -659,12 +711,35 @@
             lane = slice(b * 128, b * 128 + 128)
             two_out[at, lane] = (one[:, lane] * r * gain_two[b]).astype(jnp.bfloat16)
 
+    flush(out_one_out, one_hbm)
+    flush(two_out, two_hbm)
     for g, cols, piece in pieces(3):
         pre = dot(two_out[...], piece)
         ffn_pre[:, cols] = pre
         act[:, cols] = (pre * jax.nn.sigmoid(pre)).astype(jnp.bfloat16)
     flush(ffn_pre, ffn_hbm)
     flush(act, act_hbm)
+
+    if out_term:
+        for a in range(0, act.shape[1], 256):
+            turned_act[a : a + 256, :] = act[:, a : a + 256].T
+        n_cols, deep = out_term[-1], act.shape[1] // grid.nz
+        copies = []
+        for g in range(ng):
+            right = cot[:, g * n_cols : (g + 1) * n_cols]
+            for zt in range(grid.nz):
+                m = len(copies)
+                if m >= 4:
+                    copies[m - 4].wait()
+                stage[m % 4] = dot(turned_act[zt * deep : (zt + 1) * deep, :], right).astype(jnp.bfloat16).reshape(stage.shape[1:])
+                copies.append(
+                    pltpu.make_async_copy(stage.at[m % 4], term_hbm.at[g // grid.nc, g % grid.nc, zt], stage_sem.at[m % 4])
+                )
+                copies[m].start()
+            if g == ng // 2:
+                pump()
+        for copy in copies[-4:]:
+            copy.wait()
     for g, cols, piece in pieces(4):
         layer_out[:, cols] = (out_one_out[:, cols] + dot(act[...], piece)).astype(jnp.bfloat16)
     for _ in steps:
@@ -684,7 +759,7 @@
     return result
 
 
-def mix_forward(grid, weights, cuts, tok, tile, alive, spans, mask, dims, collective_id):
+def mix_forward(grid, weights, cuts, tok, own_params, starts, cot, dims, part, out_term, collective_id):
     rows, width = tok.shape
     nq, ng = grid.nq, grid.ng
     blocks = width // 128
@@ -695,6 +770,12 @@
     vdim, fdim, proj_dim = weights[1].shape[1] * ng, weights[3].shape[1] * ng, weights[0].shape[1] * ng
     low = jnp.bfloat16
     kept = [
+        ((rows, width), low),
+        ((rows, width), low),
+        ((rows * blocks, 128), f),
+        ((rows * blocks, 128), f),
+        ((rows, width), f),
+        ((rows, width), low),
         ((rows, proj_dim), f),
         ((rows, vdim), f),
         ((rows, vdim), f),
@@ -703,29 +784,36 @@
         ((rows, fdim), f),
         ((rows, fdim), low),
     ]
+    count_rows = 4 * dims + 3
+    tile_shape = (-(-(count_rows + 4) // 8) * 8, 128)
     local = [
-        ((rows, width), low),
-        ((rows, width), low),
-        ((rows * blocks, 128), f),
-        ((rows * blocks, 128), f),
+        ((rows, 128), f),
+        ((nq, 128), f),
         ((dims, blocks, 128), f),
-        ((4 * dims + 3, blocks, 128), f),
+        ((count_rows, blocks, 128), f),
         ((4, 128), f),
         ((rows, STRETCH), f),
-        ((rows, width), f),
-        ((rows, width), low),
         ((rows, width), low),
     ]
+    term = [jax.ShapeDtypeStruct((grid.ny, grid.nc, grid.nz, grid.nx) + out_term, low)] if out_term else []
+    held = len(term)
+    turning = [
+        pltpu.VMEM((fdim, rows), low),
+        pltpu.VMEM((4, grid.nx) + out_term, low),
+        pltpu.SemaphoreType.DMA((4,)),
+    ] if out_term else []
     result = pl.pallas_call(
-        functools.partial(mix_kernel, grid, width, dims, shapes),
-        out_shape=outs + [jax.ShapeDtypeStruct(*v) for v in local + kept],
-        in_specs=[ANY] * n + [vm] * 5,
-        out_specs=[ANY] * n + [vm] * len(local) + [ANY] * len(kept),
+        functools.partial(mix_kernel, grid, width, dims, shapes, part, out_term),
+        out_shape=outs + term + [jax.ShapeDtypeStruct(*v) for v in local + kept],
+        in_specs=[ANY] * n + [vm] * 2 + [pl.BlockSpec(memory_space=pltpu.SMEM), vm],
+        out_specs=[ANY] * (n + held) + [vm] * len(local) + [ANY] * len(kept),
         scratch_shapes=[pltpu.VMEM(*v) for v in kept]
         + [
             pltpu.VMEM((rows, vdim), low),
-            pltpu.VMEM((ng - 1,) + tile.shape, f),
-            pltpu.VMEM((nq,) + tile.shape, f),
+            pltpu.VMEM((rows, STRETCH), f),
+            pltpu.VMEM(tile_shape, f),
+            pltpu.VMEM((ng - 1,) + tile_shape, f),
+            pltpu.VMEM((nq,) + tile_shape, f),
             pltpu.VMEM((nq, dims, blocks, 128), f),
             pltpu.SemaphoreType.DMA((nq + ng - 2,)),
             pltpu.SemaphoreType.DMA((nq + ng - 2,)),
@@ -737,12 +825,13 @@
             pltpu.SemaphoreType.DMA((count,)),
             pltpu.SemaphoreType.DMA((count,)),
         ]
-        + [pltpu.VMEM((2,) + o.shape[2:], o.dtype) for o in outs],
+        + [pltpu.VMEM((2,) + o.shape[2:], o.dtype) for o in outs]
+        + turning,
         compiler_params=pltpu.CompilerParams(
             collective_id=collective_id, has_side_effects=True, vmem_limit_bytes=60 << 20
         ),
-    )(*shards, tok, tile, alive, spans, mask)
-    return result[:n], result[n:]
+    )(*shards, tok, own_params, starts, cot)
+    return result[:n], result[n : n + held], result[n + held :]
 
 
 def scan_back(grid, dims, g_rows, x_in, mixed, carry, par, alive, spans, gin_rows, before, bound, sends_b, recv_b,
@@ -972,11 +1061,11 @@
     n = len(shapes)
     zdim, vdim, fdim = sizes
     wholes, refs = refs[:n], refs[n:]
-    (cot_hbm, act_hbm, ffn_hbm, two_hbm, one_hbm, hpre_hbm, proj_hbm, att_hbm, hin_hbm, value_hbm, probs, active_hbm,
+    (first_term, cot_hbm, ffn_hbm, two_hbm, one_hbm, hpre_hbm, proj_hbm, att_hbm, hin_hbm, value_hbm, probs, active_hbm,
      normed_hbm, tok_hbm, x_hbm, mixed_hbm, carry, par, aff, alive, spans, *refs) = refs
     sums, refs = refs[:n], refs[n:]
     gtok_out, small_out, *refs = refs
-    terms, refs = refs[:n], refs[n:]
+    terms, refs = [first_term, *refs[: n - 1]], refs[n - 1 :]
     (gproj, direct, pre, bound, m_all, k_all, row_sums, two_sums, aff_sums, small, seq_in, seg_in,
      sends_b, recv_b, s_send, s_recv, own_sem, load_sem, tile_sem, stage_sem, send, recv, *scratch) = refs
     nq, ng, nc, nz = grid.nq, grid.ng, grid.nc, grid.nz
@@ -986,7 +1075,7 @@
     s = lax.axis_index("seq")
     seq_peer, seg_peer = small_peers(grid)
     meet(seq_peer + seg_peer)
-    ready = [0]
+    ready = [1]
     steps = scatter_steps(grid, shapes, terms, sums, scratch, own_sem, Sems(send, recv), lambda: ready[0])
     little = SmallSum(grid, small, small_out, seq_in, seg_in, s_send, s_recv)
     loads = [0]
@@ -995,7 +1084,7 @@
         for _ in range(count):
             next(steps, None)
 
-    pump()
+    pump(3)
     dot = functools.partial(jnp.dot, preferred_element_type=f)
 
     def dot_nt(a, b):
@@ -1041,8 +1130,6 @@
                 total = term if total is None else total + term
             if zt + 2 < nz:
                 tile(i, tiles, zt + 2).start()
-            if zt == 1:
-                pump()
             yield slice(zt * depth(i), zt * depth(i) + depth(i)), total
 
     def grads(i, left, stage, part):
@@ -1083,17 +1170,13 @@
     out_i, in_i, att_i, value_i, mix_i = range(5)
 
     def ffn_back(cot, hold, norm_grad, two):
-        wait_cot, wait_act, wait_two = fetch(cot_hbm, cot), fetch(act_hbm, hold), fetch(two_hbm, two)
-
-        def second(pre_act, left, stage, tiles):
+        wait_cot, wait_two = fetch(cot_hbm, cot), fetch(two_hbm, two)
+
+        def second(pre_act, tiles):
             begin(out_i, tiles)
             each = depth(out_i)
             pre_waits = [fetch(ffn_hbm.at[:, k * each : (k + 1) * each], pre_act.at[k]) for k in range(2)]
-            wait_act()
-            turned(hold, left)
             wait_cot()
-            grads(out_i, left, stage, cut(cot, out_i))
-            pump()
             for k, (cols, grad) in enumerate(against(out_i, tiles, cut(cot, out_i))):
                 pre_waits[k]()
                 hold[:, cols] = (grad * silu_slope(pre_act[k % 2])).astype(low)
@@ -1101,9 +1184,7 @@
                     pre_waits.append(fetch(ffn_hbm.at[:, (k + 2) * each : (k + 3) * each], pre_act.at[k % 2]))
             pump()
 
-        pl.run_scoped(
-            second, vm(2, rows, depth(out_i), kind=f), vm(fdim, rows), stage_of(out_i), pltpu.VMEM(tile_shape(out_i), low)
-        )
+        pl.run_scoped(second, vm(2, rows, depth(out_i), kind=f), pltpu.VMEM(tile_shape(out_i), low))
 
         def rest(one, hpre, upd, tok):
             waits = [fetch(one_hbm, one), fetch(hpre_hbm, hpre), fetch(proj_hbm.at[:, 0:width], upd), fetch(tok_hbm, tok)]
@@ -1299,9 +1380,9 @@
         functools.partial(layer_back_kernel, grid, dims, shapes, sizes),
         out_shape=outs
         + [jax.ShapeDtypeStruct((rows, width), jnp.bfloat16), jax.ShapeDtypeStruct(small_shape, f)]
-        + whole_shapes,
+        + whole_shapes[1:],
         in_specs=[ANY] * n + [ANY] * 10 + [vm] + [ANY] * 5 + [vm] * 5,
-        out_specs=[vm] * (n + 2) + [ANY] * n,
+        out_specs=[vm] * (n + 2) + [ANY] * (n - 1),
         scratch_shapes=[
             pltpu.VMEM((rows, width * 2 + zdim + vdim), jnp.bfloat16),
             pltpu.VMEM((rows, width), f),
@@ -1385,7 +1466,7 @@
 
 
 def backward_apart(grid, cotangent, tokens_low, forward, weights, alive, spans, sizes):
-    (normed_b, active, x_rows, mixed_rows, carry, par, affine, probs, out_one, normed_two_b, _,
+    (carry, par, affine, probs, _, normed_b, active, x_rows, mixed_rows, out_one, normed_two_b,
      projected, value_pre, attended, hidden_in, hidden_pre, ffn_hidden, ffn_act) = forward
     ffn_hidden = ffn_hidden.astype(jnp.float32)
     token_count, model_width = tokens_low.shape
@@ -1505,44 +1586,32 @@
     blocks = model_width // 128
 
     index = seq_index * ng + seg_index
-    mine = norm_gain.shape[0]
-    columns = jnp.concatenate(
-        [ema_delta.T, ema_alpha.T, ema_beta.T, ema_eta.T, norm_gain[None], ema_omega[None], ffn_gain[None]], axis=0
-    ).astype(jnp.float32)
-    count = columns.shape[0]
-    tile = jnp.zeros((-(-(count + 4) // 8) * 8, 128), jnp.float32)
-    tile = lax.dynamic_update_slice(tile, columns, (0, lax.rem(index * mine, 128)))
-    part = qk_affine.shape[0]
-    tile = lax.dynamic_update_slice(
-        tile, qk_affine.astype(jnp.float32)[None], (count + index * part // 128, lax.rem(index * part, 128))
-    )
-
-    places = jnp.arange(seq_length, dtype=jnp.int32)
-    goes_on = 1.0 - jnp.any(starts[0][None, :] == places[:, None], axis=1).astype(jnp.float32)
-    spans = jnp.broadcast_to(jnp.min(goes_on.reshape(nq, row_count), axis=1)[:, None], (nq, 128))
-    alive = lax.dynamic_slice_in_dim(goes_on, seq_index * row_count, row_count, 0)
-    alive = jnp.broadcast_to(alive[:, None], (row_count, 128))
-
-    positions_rows = seq_index * row_count + jnp.arange(row_count, dtype=jnp.int32)
-    docs_rows = jnp.sum((starts[:, None, :] <= positions_rows[None, :, None]).astype(jnp.int32), axis=2)
-    block_count = token_count // STRETCH
-    block_docs = docs_rows.reshape(block_count, STRETCH)
-    offsets = jnp.arange(STRETCH)
-    allowed = (block_docs[:, :, None] == block_docs[:, None, :]) & (offsets[:, None] >= offsets[None, :])[None]
-    mask = allowed.astype(jnp.float32).reshape(token_count, STRETCH)
+    mine, part = norm_gain.shape[0], qk_affine.shape[0]
+    own_params = [
+        ema_delta, ema_alpha, ema_beta, ema_eta, norm_gain[:, None], ema_omega[:, None], ffn_gain[:, None],
+        jnp.pad(qk_affine, (0, mine - part))[:, None],
+    ]
+    own_params = jnp.pad(jnp.concatenate(own_params, axis=1), ((0, 0), (0, 128 - 4 * dims - 4)))
+    cotangent_low = cotangent.reshape(token_count, model_width)
+    shards = [mix_weight, value_weight, out_weight, ffn_in, ffn_out]
+    apart = min(w.shape[1] for w in shards) < 128
+    out_term = None
+    if not apart:
+        k, n = ffn_out.shape
+        q = max(1, min(SCATTER_CUTS[0], k // 32))
+        out_term = (2 * q, k // (2 * q), n)
     tokens_low = tokens.reshape(token_count, model_width)
-    weights, forward = mix_forward(
-        grid, [mix_weight, value_weight, out_weight, ffn_in, ffn_out], GATHER_CUTS, tokens_low, tile, alive, spans, mask, dims, 0
-    )
-    mix_full, value_full, out_full, ffn_in_full, ffn_out_full = weights
-    (normed_b, active, x_rows, mixed_rows, carry, par, affine, probs, out_one, normed_two_b, result,
+    weights, term, forward = mix_forward(
+        grid, shards, GATHER_CUTS, tokens_low, own_params, starts, cotangent_low, dims, part, out_term, 0
+    )
+    alive, spans, *forward = forward
+    (carry, par, affine, probs, result, normed_b, active, x_rows, mixed_rows, out_one, normed_two_b,
      projected, value_pre, attended, hidden_in, hidden_pre, ffn_hidden, ffn_act) = forward
     sizes = (zdim, vdim, ffn_act.shape[1])
-    cotangent_low = cotangent.reshape(token_count, model_width)
-    if min(w.shape[1] for w in (mix_weight, value_weight, out_weight, ffn_in, ffn_out)) < 128:
+    if apart:
         result_back = backward_apart(grid, cotangent_low, tokens_low, forward, weights, alive, spans, sizes)
     else:
-        kept = [cotangent_low, ffn_act, ffn_hidden, normed_two_b, out_one, hidden_pre, projected, attended, hidden_in,
+        kept = [term[0], cotangent_low, ffn_hidden, normed_two_b, out_one, hidden_pre, projected, attended, hidden_in,
                 value_pre, active, normed_b, tokens_low, x_rows, mixed_rows]
         order = [weights[4], weights[3], weights[2], weights[1], weights[0]]
         result_back = layer_backward(

time: 430 us -> 405 us (0.942)
  Pallas kernels: 396 us -> 374 us
    pallas_call x1, Pallas kernels: 194 us -> 179 us  [layer_backward(): pl.pallas_call(functools.partial(layer_back_kernel, grid, dims, shapes, s...]
    pallas_call x1, Pallas kernels: 202 us -> 195 us  [mix_forward(): pl.pallas_call(functools.partial(mix_kernel, grid, width, dims, shapes, p...]
    unnamed x24 -> x26, local copies, waits for them, and re-layouts: 11.5 us -> 14.6 us
where the time goes in v1:
time: 405 us; the launch traced here: 397 us
  Pallas kernels  374 us (92%)
  local copies, waits for them, and re-layouts  21 us (5%)
    pallas_call x1, Pallas kernels, mix_forward(): pl.pallas_call(functools.partial(mix_kernel, grid, width, dims, shapes, p...  195 us
    pallas_call x1, Pallas kernels, layer_backward(): pl.pallas_call(functools.partial(layer_back_kernel, grid, dims, shapes, s...  179 us
    unnamed x26, local copies, waits for them, and re-layouts  14.6 us

profile of v1, /device:TPU:0, one launch (start us, length us, event | category | flops | bytes accessed | tf_op | source)
XLA Modules:
  0.0 397.2 jit_solution(1958549659214555816)
XLA Ops:
  0.6 1.8 copy.31
  2.5 0.8 copy.32
  3.2 0.8 copy.33
  4.0 0.8 copy.34
  4.8 0.8 copy.35
  5.6 0.8 copy.36
  6.3 0.8 copy.37
  7.1 0.8 copy.38
  7.8 0.7 pad_bitcast_fusion
  8.5 0.1 copy.39
  8.6 0.1 concatenate.3
  8.7 0.6 pad.9.refs_6_
  9.3 194.6 %shard_map.271 = (bf16[2,2,4,2,8,16,1056]{6,5,4,3,2,1,0:T(8,128)(2,1)}, bf16[2,2,4,2,4,32,512]{6,5,4,3,2,1,0:T(8,128)(2,1)}, bf16[2,2,4,2,4,64,256]{6,5,4,3,2,1,...) custom-call(bf16[8,16,1056]{2,1,0:T(8,128)(2,1)} %bitcast.47, ...), custom_call_target="tpu_custom_call" | custom-call | tf_op jit(solution)/shard_map/pallas_call | solution.py:805
  203.9 0.0 copy-start.3
  203.9 0.0 copy-start.4
  203.9 0.0 copy-start.5
  203.9 0.0 copy-start.6
  204.0 0.0 copy-start
  204.0 179.0 %shard_map.272 = (f32[8,64,256]{2,1,0:T(8,128)}, f32[8,16,1024]{2,1,0:T(8,128)}, f32[4,64,256]{2,1,0:T(8,128)}, f32[4,32,512]{2,1,0:T(8,128)}, f32[8,16,1056]{2,...) custom-call(bf16[2,2,4,2,8,64,256]{6,5,4,3,2,1,0:T(8,128)(2,1)} %get, ...), custom_call_target="tpu_custom_call" | custom-call | tf_op jit(solution)/shard_map/pallas_call | solution.py:1379
  382.9 0.0 copy-start.2
  383.0 0.0 copy-start.1
  383.0 1.4 dynamic-slice_bitcast_fusion.2
  384.4 0.0 copy-done.3
  384.4 0.0 copy-done.4
  384.4 0.0 copy-done.5
  384.4 0.0 copy-done.6
  384.4 1.4 subtract_multiply_fusion
  385.8 2.1 copy.40
  387.9 1.3 dynamic-slice_bitcast_fusion.5
  389.2 0.0 copy-done
  389.2 0.8 copy.47
  389.9 1.9 copy.48
  391.8 1.7 copy.49
  393.5 1.7 copy.50
  395.2 0.0 copy-done.2
  395.2 0.8 copy.51
  396.0 0.0 copy-done.1
  396.0 0.8 copy.52
Async XLA Ops:
  203.9 180.5 %copy-start.3 = (bf16[32,16]{0,1:T(8,128)(2,1)S(1)}, bf16[32,16]{0,1:T(8,128)(2,1)}, u32[]{:S(2)}) copy-start(bf16[32,16]{0,1:T(8,128)(2,1)} %param.19) | copy-start | bytes 3076
  203.9 180.5 %copy-start.4 = (bf16[32,16]{0,1:T(8,128)(2,1)S(1)}, bf16[32,16]{0,1:T(8,128)(2,1)}, u32[]{:S(2)}) copy-start(bf16[32,16]{0,1:T(8,128)(2,1)} %param.20) | copy-start | bytes 3076
  203.9 180.5 %copy-start.5 = (bf16[32,16]{0,1:T(8,128)(2,1)S(1)}, bf16[32,16]{0,1:T(8,128)(2,1)}, u32[]{:S(2)}) copy-start(bf16[32,16]{0,1:T(8,128)(2,1)} %param.21) | copy-start | bytes 3076
  203.9 180.4 %copy-start.6 = (bf16[32,16]{0,1:T(8,128)(2,1)S(1)}, bf16[32,16]{0,1:T(8,128)(2,1)}, u32[]{:S(2)}) copy-start(bf16[32,16]{0,1:T(8,128)(2,1)} %param.22) | copy-start | bytes 3076
  204.0 185.2 %copy-start = (bf16[256,1024]{1,0:T(8,128)(2,1)S(1)}, bf16[256,1024]{1,0:T(8,128)(2,1)}, u32[]{:S(2)}) copy-start(bf16[256,1024]{1,0:T(8,128)(2,1)} %get-tuple-element.47) | copy-start | bytes 1572868
  382.9 12.2 %copy-start.2 = (f32[8,16,1024]{2,1,0:T(8,128)S(1)}, f32[8,16,1024]{2,1,0:T(8,128)}, u32[]{:S(2)}) copy-start(f32[8,16,1024]{2,1,0:T(8,128)} %get-tuple-element.77) | copy-start | bytes 1572868
  383.0 13.0 %copy-start.1 = (f32[8,64,256]{2,1,0:T(8,128)S(1)}, f32[8,64,256]{2,1,0:T(8,128)}, u32[]{:S(2)}) copy-start(f32[8,64,256]{2,1,0:T(8,128)} %get-tuple-element.78) | copy-start | bytes 1572868

commit v2 on v1

--- a/solution.py
+++ b/solution.py
@@ -432,20 +432,24 @@
     return e * blocks // nq
 
 
-def place_params(grid, own, tile, count, mine, part):
+def place_params(grid, tables, vectors, affine, tile):
     index = lax.axis_index("seq") * grid.ng + lax.axis_index("seg")
-    row = lax.broadcasted_iota(jnp.int32, (mine, 128), 0)
-    lane = lax.broadcasted_iota(jnp.int32, (mine, 128), 1)
-
-    def spread(first):
-        where = (lane == row + first).astype(jnp.bfloat16)
-        return lax.dot_general(own[...], where, (((0,), (0,)), ((), ())), preferred_element_type=jnp.float32)
+
+    def spread(v):
+        mine = v.shape[1]
+        row = lax.broadcasted_iota(jnp.int32, (mine, 128), 0)
+        lane = lax.broadcasted_iota(jnp.int32, (mine, 128), 1)
+        where = (lane == row + lax.rem(index * mine, 128)).astype(jnp.bfloat16)
+        wide = jnp.broadcast_to(v.astype(jnp.float32), (max(v.shape[0], 8), mine)).astype(jnp.bfloat16)
+        return jnp.dot(wide, where, preferred_element_type=jnp.float32)[0 : v.shape[0]]
 
     tile[...] = jnp.zeros_like(tile)
-    tile[0:count, :] = spread(lax.rem(index * mine, 128))[0:count]
-    affine = spread(lax.rem(index * part, 128))[count : count + 1]
-    at = lax.broadcasted_iota(jnp.int32, (4, 128), 0) == index * part // 128
-    tile[count : count + 4, :] = jnp.where(at, affine, 0.0)
+    first = 0
+    for v in tables + vectors:
+        tile[first : first + v.shape[0], :] = spread(v[...])
+        first += v.shape[0]
+    at = lax.broadcasted_iota(jnp.int32, (4, 128), 0) == index * affine.shape[1] // 128
+    tile[first : first + 4, :] = jnp.where(at, spread(affine[...]), 0.0)
 
 
 def place_documents(grid, starts, alive, spans, mask):
@@ -471,10 +475,11 @@
     spans[...] = whole
 
 
-def mix_kernel(grid, width, dims, shapes, part, out_term, *refs):
+def mix_kernel(grid, width, dims, shapes, out_term, *refs):
     n = len(shapes)
     shards, refs = refs[:n], refs[n:]
-    tok, own_params, starts, cot, *refs = refs
+    tok, starts, cot, *refs = refs
+    tables, vectors, affine, refs = refs[:4], refs[4:7], refs[7], refs[8:]
     wholes, refs = refs[:n], refs[n:]
     term_hbm = None
     if out_term:
@@ -507,7 +512,7 @@
         copy.start()
         flushes.append(copy)
 
-    place_params(grid, own_params, tile, 4 * dims + 3, width // (nq * ng), part)
+    place_params(grid, tables, vectors, affine, tile)
     place_documents(grid, starts, alive, spans, mask)
 
     copies = []
@@ -759,7 +764,7 @@
     return result
 
 
-def mix_forward(grid, weights, cuts, tok, own_params, starts, cot, dims, part, out_term, collective_id):
+def mix_forward(grid, weights, cuts, tok, own_params, starts, cot, dims, out_term, collective_id):
     rows, width = tok.shape
     nq, ng = grid.nq, grid.ng
     blocks = width // 128
@@ -803,9 +808,9 @@
         pltpu.SemaphoreType.DMA((4,)),
     ] if out_term else []
     result = pl.pallas_call(
-        functools.partial(mix_kernel, grid, width, dims, shapes, part, out_term),
+        functools.partial(mix_kernel, grid, width, dims, shapes, out_term),
         out_shape=outs + term + [jax.ShapeDtypeStruct(*v) for v in local + kept],
-        in_specs=[ANY] * n + [vm] * 2 + [pl.BlockSpec(memory_space=pltpu.SMEM), vm],
+        in_specs=[ANY] * n + [vm, pl.BlockSpec(memory_space=pltpu.SMEM)] + [vm] * 9,
         out_specs=[ANY] * (n + held) + [vm] * len(local) + [ANY] * len(kept),
         scratch_shapes=[pltpu.VMEM(*v) for v in kept]
         + [
@@ -830,7 +835,7 @@
         compiler_params=pltpu.CompilerParams(
             collective_id=collective_id, has_side_effects=True, vmem_limit_bytes=60 << 20
         ),
-    )(*shards, tok, own_params, starts, cot)
+    )(*shards, tok, starts, cot, *own_params)
     return result[:n], result[n : n + held], result[n + held :]
 
 
@@ -1588,10 +1593,8 @@
     index = seq_index * ng + seg_index
     mine, part = norm_gain.shape[0], qk_affine.shape[0]
     own_params = [
-        ema_delta, ema_alpha, ema_beta, ema_eta, norm_gain[:, None], ema_omega[:, None], ffn_gain[:, None],
-        jnp.pad(qk_affine, (0, mine - part))[:, None],
+        ema_delta.T, ema_alpha.T, ema_beta.T, ema_eta.T, norm_gain[None], ema_omega[None], ffn_gain[None], qk_affine[None]
     ]
-    own_params = jnp.pad(jnp.concatenate(own_params, axis=1), ((0, 0), (0, 128 - 4 * dims - 4)))
     cotangent_low = cotangent.reshape(token_count, model_width)
     shards = [mix_weight, value_weight, out_weight, ffn_in, ffn_out]
     apart = min(w.shape[1] for w in shards) < 128
@@ -1602,7 +1605,7 @@
         out_term = (2 * q, k // (2 * q), n)
     tokens_low = tokens.reshape(token_count, model_width)
     weights, term, forward = mix_forward(
-        grid, shards, GATHER_CUTS, tokens_low, own_params, starts, cotangent_low, dims, part, out_term, 0
+        grid, shards, GATHER_CUTS, tokens_low, own_params, starts, cotangent_low, dims, out_term, 0
     )
     alive, spans, *forward = forward
     (carry, par, affine, probs, result, normed_b, active, x_rows, mixed_rows, out_one, normed_two_b,

time: 405 us -> 398 us (0.983)
  local copies, waits for them, and re-layouts: 21 us -> 14.2 us
    unnamed x26 -> x22, local copies, waits for them, and re-layouts: 14.6 us -> 11.5 us
where the time goes in v2:
time: 398 us; the launch traced here: 391 us
  Pallas kernels  374 us (94%)
  local copies, waits for them, and re-layouts  14.2 us (4%)
    pallas_call x1, Pallas kernels, mix_forward(): pl.pallas_call(functools.partial(mix_kernel, grid, width, dims, shapes, o...  195 us
    pallas_call x1, Pallas kernels, layer_backward(): pl.pallas_call(functools.partial(layer_back_kernel, grid, dims, shapes, s...  179 us
    unnamed x22, local copies, waits for them, and re-layouts  11.5 us

profile of v2, /device:TPU:0, one launch (start us, length us, event | category | flops | bytes accessed | tf_op | source)
XLA Modules:
  0.0 390.6 jit_solution(18245489334864520355)
XLA Ops:
  0.6 1.8 copy.31
  2.5 194.7 %shard_map.271 = (bf16[2,2,4,2,8,16,1056]{6,5,4,3,2,1,0:T(8,128)(2,1)}, bf16[2,2,4,2,4,32,512]{6,5,4,3,2,1,0:T(8,128)(2,1)}, bf16[2,2,4,2,4,64,256]{6,5,4,3,2,1,...) custom-call(bf16[8,16,1056]{2,1,0:T(8,128)(2,1)} %bitcast.50, ...), custom_call_target="tpu_custom_call" | custom-call | tf_op jit(solution)/shard_map/pallas_call | solution.py:810
  197.2 0.0 copy-start.3
  197.2 0.0 copy-start.4
  197.2 0.0 copy-start.5
  197.2 0.0 copy-start.6
  197.3 0.0 copy-start
  197.3 179.1 %shard_map.272 = (f32[8,64,256]{2,1,0:T(8,128)}, f32[8,16,1024]{2,1,0:T(8,128)}, f32[4,64,256]{2,1,0:T(8,128)}, f32[4,32,512]{2,1,0:T(8,128)}, f32[8,16,1056]{2,...) custom-call(bf16[2,2,4,2,8,64,256]{6,5,4,3,2,1,0:T(8,128)(2,1)} %get, ...), custom_call_target="tpu_custom_call" | custom-call | tf_op jit(solution)/shard_map/pallas_call | solution.py:1384
  376.3 0.0 copy-start.2
  376.3 0.0 copy-start.1
  376.4 1.4 dynamic-slice_bitcast_fusion.2
  377.8 0.0 copy-done.3
  377.8 0.0 copy-done.4
  377.8 0.0 copy-done.5
  377.8 0.0 copy-done.6
  377.8 1.4 subtract_multiply_fusion
  379.2 2.1 copy.32
  381.3 1.3 dynamic-slice_bitcast_fusion.5
  382.5 0.0 copy-done
  382.5 0.8 copy.39
  383.3 1.9 copy.40
  385.2 1.7 copy.41
  386.9 1.7 copy.42
  388.5 0.0 copy-done.2
  388.5 0.8 copy.43
  389.3 0.0 copy-done.1
  389.3 0.8 copy.44
Async XLA Ops:
  197.2 180.6 %copy-start.3 = (bf16[32,16]{0,1:T(8,128)(2,1)S(1)}, bf16[32,16]{0,1:T(8,128)(2,1)}, u32[]{:S(2)}) copy-start(bf16[32,16]{0,1:T(8,128)(2,1)} %param.19) | copy-start | bytes 3076
  197.2 180.5 %copy-start.4 = (bf16[32,16]{0,1:T(8,128)(2,1)S(1)}, bf16[32,16]{0,1:T(8,128)(2,1)}, u32[]{:S(2)}) copy-start(bf16[32,16]{0,1:T(8,128)(2,1)} %param.20) | copy-start | bytes 3076
  197.2 180.5 %copy-start.5 = (bf16[32,16]{0,1:T(8,128)(2,1)S(1)}, bf16[32,16]{0,1:T(8,128)(2,1)}, u32[]{:S(2)}) copy-start(bf16[32,16]{0,1:T(8,128)(2,1)} %param.21) | copy-start | bytes 3076
  197.2 180.5 %copy-start.6 = (bf16[32,16]{0,1:T(8,128)(2,1)S(1)}, bf16[32,16]{0,1:T(8,128)(2,1)}, u32[]{:S(2)}) copy-start(bf16[32,16]{0,1:T(8,128)(2,1)} %param.22) | copy-start | bytes 3076
  197.3 185.3 %copy-start = (bf16[256,1024]{1,0:T(8,128)(2,1)S(1)}, bf16[256,1024]{1,0:T(8,128)(2,1)}, u32[]{:S(2)}) copy-start(bf16[256,1024]{1,0:T(8,128)(2,1)} %get-tuple-element.47) | copy-start | bytes 1572868
  376.3 12.2 %copy-start.2 = (f32[8,16,1024]{2,1,0:T(8,128)S(1)}, f32[8,16,1024]{2,1,0:T(8,128)}, u32[]{:S(2)}) copy-start(f32[8,16,1024]{2,1,0:T(8,128)} %get-tuple-element.77) | copy-start | bytes 1572868
  376.3 13.0 %copy-start.1 = (f32[8,64,256]{2,1,0:T(8,128)S(1)}, f32[8,64,256]{2,1,0:T(8,128)}, u32[]{:S(2)}) copy-start(f32[8,64,256]{2,1,0:T(8,128)} %get-tuple-element.78) | copy-start | bytes 1572868

commit v3 on v2

--- a/solution.py
+++ b/solution.py
@@ -157,7 +157,7 @@
         if j == 4:
             finish(core_waits[k])
             at[j] += 1
-            return [i] if q + 1 == shapes[i][0] // 2 else []
+            return [(i, q), i] if q + 1 == shapes[i][0] // 2 else [(i, q)]
         for h in (0, 1):
             if j:
                 finish(got[k, h])
@@ -432,6 +432,10 @@
     return e * blocks // nq
 
 
+def by_cut(shape):
+    return 2 * shape[1] % 128 == 0
+
+
 def place_params(grid, tables, vectors, affine, tile):
     index = lax.axis_index("seq") * grid.ng + lax.axis_index("seg")
 
@@ -488,7 +492,7 @@
      normed_hbm, active_hbm, x_hbm, mixed_hbm, one_hbm, two_hbm, proj_hbm, value_hbm, att_hbm, hin_hbm, hpre_hbm, ffn_hbm, act_hbm,
      normed_out, active_out, x_out, mixed_out, out_one_out, two_out, proj, value_pre, att, hin, hpre, ffn_pre, act, values,
      mask, tile, tiles, table, bound, sends_t, recv_t, sends_b, recv_b, own_sem, flush_sem, load_sem, send, recv,
-     *slots) = refs
+     layer_sum, *slots) = refs
     if out_term:
         *slots, turned_act, stage, stage_sem = slots
     nq, ng = grid.nq, grid.ng
@@ -745,8 +749,25 @@
                 pump()
         for copy in copies[-4:]:
             copy.wait()
-    for g, cols, piece in pieces(4):
-        layer_out[:, cols] = (out_one_out[:, cols] + dot(act[...], piece)).astype(jnp.bfloat16)
+    cuts, high, n_cols = shapes[4]
+    if by_cut(shapes[4]):
+        layer_sum[...] = out_one_out[...]
+        deep, each = cuts * high, 2 * high
+        for q in range(cuts // 2):
+            while (4, q) not in done:
+                pump()
+            slot = slots[4].at[q % 2]
+            copy = pltpu.make_async_copy(wholes[4].at[:, :, :, :, 2 * q : 2 * q + 2], slot, load_sem.at[4, q % 2])
+            copy.start()
+            left = jnp.concatenate([act[:, a * deep + q * each : a * deep + (q + 1) * each] for a in range(nq)], axis=1)
+            copy.wait()
+            for g in range(ng):
+                cols = slice(g * n_cols, (g + 1) * n_cols)
+                layer_sum[:, cols] += dot(left, slots[4][q % 2, g // grid.nc, g % grid.nc].reshape(-1, n_cols))
+        layer_out[...] = layer_sum[...].astype(jnp.bfloat16)
+    else:
+        for g, cols, piece in pieces(4):
+            layer_out[:, cols] = (out_one_out[:, cols] + dot(act[...], piece)).astype(jnp.bfloat16)
     for _ in steps:
         pass
     for copy in flushes:
@@ -830,7 +851,9 @@
             pltpu.SemaphoreType.DMA((count,)),
             pltpu.SemaphoreType.DMA((count,)),
         ]
-        + [pltpu.VMEM((2,) + o.shape[2:], o.dtype) for o in outs]
+        + [pltpu.VMEM((rows, width), f)]
+        + [pltpu.VMEM((2,) + o.shape[2:], o.dtype) for o in outs[:4]]
+        + [pltpu.VMEM((2,) + (outs[4].shape[:4] + (2,) + outs[4].shape[5:] if by_cut(shapes[4]) else outs[4].shape[2:]), low)]
         + turning,
         compiler_params=pltpu.CompilerParams(
             collective_id=collective_id, has_side_effects=True, vmem_limit_bytes=60 << 20

time: 398 us -> 397 us (level)
  no operation moved by 1% of the time
where the time goes in v3:
time: 397 us; the launch traced here: 390 us
  Pallas kernels  373 us (94%)
  local copies, waits for them, and re-layouts  14.2 us (4%)
    pallas_call x1, Pallas kernels, mix_forward(): pl.pallas_call(functools.partial(mix_kernel, grid, width, dims, shapes, o...  194 us
    pallas_call x1, Pallas kernels, layer_backward(): pl.pallas_call(functools.partial(layer_back_kernel, grid, dims, shapes, s...  179 us
    unnamed x22, local copies, waits for them, and re-layouts  11.5 us

profile of v3, /device:TPU:0, one launch (start us, length us, event | category | flops | bytes accessed | tf_op | source)
XLA Modules:
  0.0 389.9 jit_solution(8152436605598181684)
XLA Ops:
  0.6 1.8 copy.31
  2.5 194.2 %shard_map.271 = (bf16[2,2,4,2,8,16,1056]{6,5,4,3,2,1,0:T(8,128)(2,1)}, bf16[2,2,4,2,4,32,512]{6,5,4,3,2,1,0:T(8,128)(2,1)}, bf16[2,2,4,2,4,64,256]{6,5,4,3,2,1,...) custom-call(bf16[8,16,1056]{2,1,0:T(8,128)(2,1)} %bitcast.50, ...), custom_call_target="tpu_custom_call" | custom-call | tf_op jit(solution)/shard_map/pallas_call | solution.py:831
  196.7 0.0 copy-start.3
  196.7 0.0 copy-start.4
  196.7 0.0 copy-start.5
  196.7 0.0 copy-start.6
  196.7 0.0 copy-start
  196.8 178.9 %shard_map.272 = (f32[8,64,256]{2,1,0:T(8,128)}, f32[8,16,1024]{2,1,0:T(8,128)}, f32[4,64,256]{2,1,0:T(8,128)}, f32[4,32,512]{2,1,0:T(8,128)}, f32[8,16,1056]{2,...) custom-call(bf16[2,2,4,2,8,64,256]{6,5,4,3,2,1,0:T(8,128)(2,1)} %get, ...), custom_call_target="tpu_custom_call" | custom-call | tf_op jit(solution)/shard_map/pallas_call | solution.py:1407
  375.6 0.0 copy-start.2
  375.6 0.0 copy-start.1
  375.6 1.4 dynamic-slice_bitcast_fusion.2
  377.0 0.0 copy-done.3
  377.0 0.0 copy-done.4
  377.1 0.0 copy-done.5
  377.1 0.0 copy-done.6
  377.1 1.4 subtract_multiply_fusion
  378.5 2.1 copy.32
  380.6 1.3 dynamic-slice_bitcast_fusion.5
  381.8 0.0 copy-done
  381.8 0.8 copy.39
  382.6 1.9 copy.40
  384.5 1.7 copy.41
  386.2 1.7 copy.42
  387.8 0.0 copy-done.2
  387.8 0.8 copy.43
  388.6 0.0 copy-done.1
  388.6 0.8 copy.44
Async XLA Ops:
  196.7 180.4 %copy-start.3 = (bf16[32,16]{0,1:T(8,128)(2,1)S(1)}, bf16[32,16]{0,1:T(8,128)(2,1)}, u32[]{:S(2)}) copy-start(bf16[32,16]{0,1:T(8,128)(2,1)} %param.19) | copy-start | bytes 3076
  196.7 180.3 %copy-start.4 = (bf16[32,16]{0,1:T(8,128)(2,1)S(1)}, bf16[32,16]{0,1:T(8,128)(2,1)}, u32[]{:S(2)}) copy-start(bf16[32,16]{0,1:T(8,128)(2,1)} %param.20) | copy-start | bytes 3076
  196.7 180.3 %copy-start.5 = (bf16[32,16]{0,1:T(8,128)(2,1)S(1)}, bf16[32,16]{0,1:T(8,128)(2,1)}, u32[]{:S(2)}) copy-start(bf16[32,16]{0,1:T(8,128)(2,1)} %param.21) | copy-start | bytes 3076
  196.7 180.3 %copy-start.6 = (bf16[32,16]{0,1:T(8,128)(2,1)S(1)}, bf16[32,16]{0,1:T(8,128)(2,1)}, u32[]{:S(2)}) copy-start(bf16[32,16]{0,1:T(8,128)(2,1)} %param.22) | copy-start | bytes 3076
  196.7 185.1 %copy-start = (bf16[256,1024]{1,0:T(8,128)(2,1)S(1)}, bf16[256,1024]{1,0:T(8,128)(2,1)}, u32[]{:S(2)}) copy-start(bf16[256,1024]{1,0:T(8,128)(2,1)} %get-tuple-element.47) | copy-start | bytes 1572868
  375.6 12.2 %copy-start.2 = (f32[8,16,1024]{2,1,0:T(8,128)S(1)}, f32[8,16,1024]{2,1,0:T(8,128)}, u32[]{:S(2)}) copy-start(f32[8,16,1024]{2,1,0:T(8,128)} %get-tuple-element.77) | copy-start | bytes 1572868
  375.6 13.0 %copy-start.1 = (f32[8,64,256]{2,1,0:T(8,128)S(1)}, f32[8,64,256]{2,1,0:T(8,128)}, u32[]{:S(2)}) copy-start(f32[8,64,256]{2,1,0:T(8,128)} %get-tuple-element.78) | copy-start | bytes 1572868
